TPU v7x, 32 devices: a whole 2x2x4 slice. The times are simulated.
32 devices in a mesh: freq: 2 (over y), bfly: 16 (over z, x, core).
Axes of the slice: x: 2, y: 2, z: 4, core: 2. Of those that a mesh axis runs over, the one named last changes fastest.
Arguments:
- coefficients: bfloat16 [32768, 512], P(('freq', 'bfly')), parts along dimension 0, may hold values from -6 to 6
- transfer: bfloat16 [5, 32768, 1024], P(None, ('freq', 'bfly')), parts along dimension 1, may hold values from -0.25 to 0.25
- ranks: int32 [6, 16], P(None, 'bfly'), may hold values from 256 to 1024, as said below
- owner_map: int32 [16], replicated, may hold values from 0 to 3, as said below
Outputs:
- target_field: bfloat16 [8192, 512], P(('freq', 'bfly')), parts along dimension 0
There are 2 independent parts, one for each index of `freq`. A program takes and returns all parts, laid end to end along the dimension named above; an argument that names none is the same for every part. Nothing has to cross between parts.
Inputs may be any that keep to these rules, and one draw needn't show every extreme that they name: Every row of ranks holds the value 1024 at least once. `owner_map`: within each aligned group of four blocks the four entries are a permutation of 0 to 3.
All inputs are finite; a program needn't handle non-finite values.
Results may differ from a plain program's by a relative error of at most 0.0095.
Values may be sent and summed in bfloat16 or wider, within the bound.
No kernel may reach another device: no remote copies, remote signals or barrier semaphores. Data moves between devices by JAX's collectives and lax.ppermute only.
A program may use at most 64 MiB of HBM per device.

v0:
```python
import jax
import jax.numpy as jnp
from jax import lax
from jax.sharding import PartitionSpec as P

R = 1024
W = 512
LEVELS = 5


def from_partner(value, axis, apart):
    mask = 2**apart
    pairs = [(source, source ^ mask) for source in range(lax.axis_size(axis))]
    return lax.ppermute(value, axis, pairs)


def shards(coefficients, transfer, ranks, owner_map):
    half_rows = R // 2
    quarter = R // 4
    count = lax.axis_size("bfly")
    log_count = count.bit_length() - 1
    position = lax.axis_index("bfly")
    row_ids = jnp.arange(R, dtype=jnp.int32)
    current = jnp.where((row_ids < ranks[0, 0])[:, None], coefficients, jnp.zeros((), jnp.bfloat16))
    for level_idx in range(LEVELS):
        bit_pos = (log_count - 1 - level_idx) % log_count
        which_half = position >> bit_pos & 1
        paired_rows = current.reshape(half_rows, 2, W)
        own_half = lax.dynamic_index_in_dim(paired_rows, which_half, 1, keepdims=False)
        other_half = lax.dynamic_index_in_dim(paired_rows, 1 - which_half, 1, keepdims=False)
        received = from_partner(other_half, "bfly", bit_pos)
        matrix = transfer[level_idx]
        own_cols = lax.dynamic_slice_in_dim(matrix, which_half * half_rows, half_rows, 1)
        peer_cols = lax.dynamic_slice_in_dim(matrix, (1 - which_half) * half_rows, half_rows, 1)
        product = jnp.dot(own_cols, own_half, preferred_element_type=jnp.float32)
        product = product + jnp.dot(peer_cols, received, preferred_element_type=jnp.float32)
        keep_rows = (row_ids < ranks[level_idx + 1, 0])[:, None]
        current = jnp.where(keep_rows, product, jnp.float32(0.0)).astype(jnp.bfloat16)
    group_pos = position % 4
    group_idx = position // 4
    owners = lax.dynamic_slice_in_dim(owner_map, group_idx * 4, 4, 0)
    mine = owners[group_pos]
    quarters = current.reshape(4, quarter, W)

    def select_quarter(index):
        return lax.dynamic_index_in_dim(quarters, index, 0, keepdims=False)

    pair_mate = owners[group_pos ^ 1]
    far_first = owners[group_pos ^ 2]
    far_second = owners[group_pos ^ 3]
    outgoing = jnp.stack([select_quarter(far_first), select_quarter(far_second)])
    kept_pair = jnp.stack([select_quarter(mine), select_quarter(pair_mate)])
    incoming = from_partner(outgoing, "bfly", 1)
    partial_value = kept_pair.astype(jnp.float32) + incoming.astype(jnp.float32)
    mate_sum = from_partner(partial_value[1].astype(jnp.bfloat16), "bfly", 0).astype(jnp.float32)
    total = partial_value[0] + mate_sum
    return total.astype(jnp.bfloat16)


def solution(mesh):
    in_specs = (P(("freq", "bfly"), None), P(None, ("freq", "bfly"), None), P(None, "bfly"), P())
    out_specs = P(("freq", "bfly"), None)
    return jax.shard_map(shards, mesh=mesh, in_specs=in_specs, out_specs=out_specs, check_vma=False)
```

profile of v0, /device:TPU:0, one launch (start us, length us, event | category | flops | bytes accessed | tf_op | source)
XLA Modules:
  0.0 135.5 jit_solution(16034869629172434246)
XLA Ops:
  0.0 1.5 %fusion.42 = (s32[1,1]{0,1:T(1,128)}, s32[1,1]{0,1:T(1,128)}, s32[1,1]{0,1:T(1,128)}, s32[1,1]{0,1:T(1,128)}, s32[1,1]{0,1:T(1,128)}, /*index=5*/s32[1,1]{0,1:T(1,128)}) fusion(s32[6,1]{0,1:T(1,128)} %param.6), kind=kLoop, calls=%fused_computation.81 | loop fusion | bytes 48 | tf_op jit(solution)/shard_map/slice | solution.py:37
  1.5 0.6 iota_compare_fusion
  2.1 1.4 %broadcast_select_fusion = bf16[1024,512]{1,0:T(8,128)(2,1)S(1)} fusion(bf16[1024,512]{1,0:T(8,128)(2,1)} %param.4, pred[1024]{0:T(1024)(128)(4,1)S(1)} %iota_compare_fusion), kind=kLoop, calls=%fused_computation.31 | loop fusion | flops 524288 | bytes 2098176 | tf_op jit(solution)/shard_map/jit(_where)/select_n | solution.py:24
  3.5 0.4 reshape.53
  4.0 2.2 %constant_dynamic-slice_fusion.12 = (bf16[512,1,512]{2,1,0:T(2,128)(2,1)S(1)}, bf16[512,1,512]{2,1,0:T(2,128)(2,1)S(1)}) fusion(bf16[512,2,512]{2,1,0:T(2,128)(2,1)S(1)} %reshape.53, s32[]{:T(128)S(6)} %select_n.129, s32[]{:T(128)S(6)} %select_n.127), kind=kLoop, calls=%fused_computation.65 | loop fusion | bytes 2097160 | tf_op jit(solution)/shard_map/jit(dynamic_index_in_dim)/dynamic_slice | solution.py:30
  6.1 0.9 copy.52
  7.1 4.0 %collective-permute-start = (bf16[512,512]{1,0:T(8,128)(2,1)}, bf16[512,512]{1,0:T(8,128)(2,1)}, u32[]{:S(2)}, u32[]{:S(2)}) collective-permute-start(bf16[512,512]{1,0:T(8,128)(2,1)} %bitcast.83), channel_id=1, source_target_pairs={{0,8},{1,9},{2,10},{3,11},{4,12},{5,13},{6,14},{7,15},{8,0},{9,1},... | collective-permute-start | bytes 1572872 | tf_op jit(solution)/shard_map/ppermute | solution.py:14
  11.1 7.4 %fusion.40 = (bf16[1,1024,1024]{2,1,0:T(8,128)(2,1)}, bf16[1,1024,1024]{2,1,0:T(8,128)(2,1)}, bf16[1,1024,1024]{2,1,0:T(8,128)(2,1)}, bf16[1,1024,1024]{2,1,0:T(8,128)(2,1)S(1)}, bf16[1,1024,1024]{2,1,0:T(8,128)(2,1)}) fusion(bf16[5,1024,1024]{2,1,0:T(8,128)(2,1)} %param.5), kind=kLoop, calls=%fused_computation.79 | loop fusion | bytes 20971520 | tf_op jit(solution)/shard_map/slice | solution.py:32
  18.5 0.0 copy-start.3
  18.5 0.7 iota_compare_fusion.1
  19.3 1.9 %fusion.5 = f32[1024,512]{1,0:T(8,128)S(1)} fusion(bf16[1,1024,1024]{2,1,0:T(8,128)(2,1)} %get-tuple-element.5, s32[]{:T(128)S(6)} %select_n.122, bf16[512,1,512]{2,1,0:T(2,128)(2,1)S(1)} %get-tuple-element.23), kind=kOutput, calls=%fused_computation.10 | convolution fusion | flops 536870912 | bytes 3670020 | tf_op jit(solution)/shard_map/dot_general | solution.py:35
  21.2 13.4 %collective-permute-done = bf16[512,512]{1,0:T(8,128)(2,1)} collective-permute-done((bf16[512,512]{1,0:T(8,128)(2,1)}, bf16[512,512]{1,0:T(8,128)(2,1)}, u32[]{:S(2)}, u32[]{:S(2)}) %collective-permute-start) | collective-permute-done | bytes 524320 | tf_op jit(solution)/shard_map/ppermute | solution.py:14
  34.6 0.0 copy-done.3
  34.6 2.7 %select_convert_fusion.4 = bf16[1024,512]{1,0:T(8,128)(2,1)} fusion(f32[1024,512]{1,0:T(8,128)S(1)} %fusion.5, bf16[512,512]{1,0:T(8,128)(2,1)} %collective-permute-done, bf16[1,1024,1024]{2,1,0:T(8,128)(2,1)S(1)} %copy-done.3, s32[]{:T(128)S(6)} %select_n.128, pred[1024]{0:T(1024)(128)(4,1)S(1)} %iota_compare_fusion.1), kind=kOutput, calls=%fused_computation.4 | convolution fusion | flops 538443776 | bytes 4719620 | tf_op jit(solution)/shard_map/dot_general | solution.py:36
  37.3 1.5 %reshape.54 = bf16[512,2,512]{2,1,0:T(2,128)(2,1)S(1)} reshape(bf16[1024,512]{1,0:T(8,128)(2,1)} %select_convert_fusion.4) | data formatting | bytes 2097152 | tf_op jit(solution)/shard_map/reshape | solution.py:28
  38.8 3.1 %constant_dynamic-slice_fusion.10 = (bf16[512,1,512]{2,1,0:T(2,128)(2,1)S(1)}, bf16[512,1,512]{2,1,0:T(2,128)(2,1)}) fusion(bf16[512,2,512]{2,1,0:T(2,128)(2,1)S(1)} %reshape.54, s32[]{:T(128)S(6)} %select_n.133, s32[]{:T(128)S(6)} %select_n.131), kind=kLoop, calls=%fused_computation.62 | loop fusion | bytes 2097160 | tf_op jit(solution)/shard_map/jit(dynamic_index_in_dim)/dynamic_slice | solution.py:30
  41.9 0.1 copy.51
  42.1 0.8 collective-permute-start.1
  42.9 0.0 copy-start.2
  42.9 0.8 iota_compare_fusion.2
  43.6 2.3 %fusion.7 = f32[1024,512]{1,0:T(8,128)S(1)} fusion(bf16[1,1024,1024]{2,1,0:T(8,128)(2,1)} %get-tuple-element.9, s32[]{:T(128)S(6)} %select_n.125, bf16[512,1,512]{2,1,0:T(2,128)(2,1)} %get-tuple-element.21), kind=kOutput, calls=%fused_computation.12 | convolution fusion | flops 536870912 | bytes 4194308 | tf_op jit(solution)/shard_map/dot_general | solution.py:35
  45.9 9.3 %collective-permute-done.1 = bf16[512,512]{1,0:T(8,128)(2,1)S(1)} collective-permute-done((bf16[512,512]{1,0:T(8,128)(2,1)S(1)}, bf16[512,512]{1,0:T(8,128)(2,1)S(1)}, u32[]{:S(2)}, u32[]{:S(2)}) %collective-permute-start.1) | collective-permute-done | bytes 524320 | tf_op jit(solution)/shard_map/ppermute | solution.py:14
  55.2 0.0 copy-done.2
  55.2 1.7 %select_convert_fusion.3 = bf16[1024,512]{1,0:T(8,128)(2,1)} fusion(f32[1024,512]{1,0:T(8,128)S(1)} %fusion.7, bf16[512,512]{1,0:T(8,128)(2,1)S(1)} %collective-permute-done.1, bf16[1,1024,1024]{2,1,0:T(8,128)(2,1)S(1)} %copy-done.2, s32[]{:T(128)S(6)} %select_n.132, pred[1024]{0:T(1024)(128)(4,1)S(1)} %iota_compare_fusion.2), kind=kOutput, calls=%fused_computation.3 | convolution fusion | flops 538443776 | bytes 4719620 | tf_op jit(solution)/shard_map/dot_general | solution.py:36
  57.0 1.6 %reshape.55 = bf16[512,2,512]{2,1,0:T(2,128)(2,1)S(1)} reshape(bf16[1024,512]{1,0:T(8,128)(2,1)} %select_convert_fusion.3) | data formatting | bytes 2097152 | tf_op jit(solution)/shard_map/reshape | solution.py:28
  58.6 3.1 %constant_dynamic-slice_fusion.8 = (bf16[512,1,512]{2,1,0:T(2,128)(2,1)S(1)}, bf16[512,1,512]{2,1,0:T(2,128)(2,1)}) fusion(bf16[512,2,512]{2,1,0:T(2,128)(2,1)S(1)} %reshape.55, s32[]{:T(128)S(6)} %select_n.137, s32[]{:T(128)S(6)} %select_n.135), kind=kLoop, calls=%fused_computation.59 | loop fusion | bytes 2097160 | tf_op jit(solution)/shard_map/jit(dynamic_index_in_dim)/dynamic_slice | solution.py:30
  61.8 0.1 copy.50
  61.9 1.3 collective-permute-start.2
  63.2 0.0 copy-start.1
  63.2 0.8 iota_compare_fusion.3
  64.0 2.3 %fusion.9 = f32[1024,512]{1,0:T(8,128)S(1)} fusion(bf16[1,1024,1024]{2,1,0:T(8,128)(2,1)} %get-tuple-element.6, s32[]{:T(128)S(6)} %select_n.124, bf16[512,1,512]{2,1,0:T(2,128)(2,1)} %get-tuple-element.19), kind=kOutput, calls=%fused_computation.14 | convolution fusion | flops 536870912 | bytes 4194308 | tf_op jit(solution)/shard_map/dot_general | solution.py:35
  66.2 7.9 %collective-permute-done.2 = bf16[512,512]{1,0:T(8,128)(2,1)S(1)} collective-permute-done((bf16[512,512]{1,0:T(8,128)(2,1)S(1)}, bf16[512,512]{1,0:T(8,128)(2,1)S(1)}, u32[]{:S(2)}, u32[]{:S(2)}) %collective-permute-start.2) | collective-permute-done | bytes 524320 | tf_op jit(solution)/shard_map/ppermute | solution.py:14
  74.1 0.0 copy-done.1
  74.1 1.7 %select_convert_fusion.2 = bf16[1024,512]{1,0:T(8,128)(2,1)} fusion(f32[1024,512]{1,0:T(8,128)S(1)} %fusion.9, bf16[512,512]{1,0:T(8,128)(2,1)S(1)} %collective-permute-done.2, bf16[1,1024,1024]{2,1,0:T(8,128)(2,1)S(1)} %copy-done.1, s32[]{:T(128)S(6)} %select_n.136, pred[1024]{0:T(1024)(128)(4,1)S(1)} %iota_compare_fusion.3), kind=kOutput, calls=%fused_computation.2 | convolution fusion | flops 538443776 | bytes 4719620 | tf_op jit(solution)/shard_map/dot_general | solution.py:36
  75.8 1.5 %reshape.56 = bf16[512,2,512]{2,1,0:T(2,128)(2,1)S(1)} reshape(bf16[1024,512]{1,0:T(8,128)(2,1)} %select_convert_fusion.2) | data formatting | bytes 2097152 | tf_op jit(solution)/shard_map/reshape | solution.py:28
  77.3 3.1 %constant_dynamic-slice_fusion.6 = (bf16[512,1,512]{2,1,0:T(2,128)(2,1)S(1)}, bf16[512,1,512]{2,1,0:T(2,128)(2,1)}) fusion(bf16[512,2,512]{2,1,0:T(2,128)(2,1)S(1)} %reshape.56, s32[]{:T(128)S(6)} %select_n.141, s32[]{:T(128)S(6)} %select_n.139), kind=kLoop, calls=%fused_computation.56 | loop fusion | bytes 2097160 | tf_op jit(solution)/shard_map/jit(dynamic_index_in_dim)/dynamic_slice | solution.py:30
  80.5 0.1 copy.49
  80.6 0.1 collective-permute-start.3
  80.7 0.0 copy-start
  80.7 0.7 iota_compare_fusion.4
  81.4 2.3 %fusion.11 = f32[1024,512]{1,0:T(8,128)S(1)} fusion(bf16[1,1024,1024]{2,1,0:T(8,128)(2,1)} %get-tuple-element.7, s32[]{:T(128)S(6)} %select_n.123, bf16[512,1,512]{2,1,0:T(2,128)(2,1)} %get-tuple-element.17), kind=kOutput, calls=%fused_computation.16 | convolution fusion | flops 536870912 | bytes 4194308 | tf_op jit(solution)/shard_map/dot_general | solution.py:35
  83.7 0.0 collective-permute-done.3
  83.7 0.0 copy-done
  83.7 1.7 %select_convert_fusion.1 = bf16[1024,512]{1,0:T(8,128)(2,1)} fusion(f32[1024,512]{1,0:T(8,128)S(1)} %fusion.11, bf16[512,512]{1,0:T(8,128)(2,1)S(1)} %collective-permute-done.3, bf16[1,1024,1024]{2,1,0:T(8,128)(2,1)S(1)} %copy-done, s32[]{:T(128)S(6)} %select_n.140, pred[1024]{0:T(1024)(128)(4,1)S(1)} %iota_compare_fusion.4), kind=kOutput, calls=%fused_computation.1 | convolution fusion | flops 538443776 | bytes 4719620 | tf_op jit(solution)/shard_map/dot_general | solution.py:36
  85.4 1.5 %reshape.57 = bf16[512,2,512]{2,1,0:T(2,128)(2,1)S(1)} reshape(bf16[1024,512]{1,0:T(8,128)(2,1)} %select_convert_fusion.1) | data formatting | bytes 2097152 | tf_op jit(solution)/shard_map/reshape | solution.py:28
  86.9 0.0 copy-start.4
  86.9 3.2 %constant_dynamic-slice_fusion.4 = (bf16[512,1,512]{2,1,0:T(2,128)(2,1)S(1)}, bf16[512,1,512]{2,1,0:T(2,128)(2,1)}) fusion(bf16[512,2,512]{2,1,0:T(2,128)(2,1)S(1)} %reshape.57, s32[]{:T(128)S(6)} %select_n.129, s32[]{:T(128)S(6)} %select_n.127), kind=kLoop, calls=%fused_computation.53 | loop fusion | bytes 2097160 | tf_op jit(solution)/shard_map/jit(dynamic_index_in_dim)/dynamic_slice | solution.py:30
  90.1 0.1 copy.48
  90.2 4.3 %collective-permute-start.4 = (bf16[512,512]{1,0:T(8,128)(2,1)S(1)}, bf16[512,512]{1,0:T(8,128)(2,1)S(1)}, u32[]{:S(2)}, u32[]{:S(2)}) collective-permute-start(bf16[512,512]{1,0:T(8,128)(2,1)S(1)} %bitcast.85), channel_id=1, source_target_pairs={{0,8},{1,9},{2,10},{3,11},{4,12},{5,13},{6,14},{7,15},{8,0},{9,1},... | collective-permute-start | bytes 1572872 | tf_op jit(solution)/shard_map/ppermute | solution.py:14
  94.5 0.0 copy-done.4
  94.5 0.7 fusion.41
  102.6 0.7 iota_compare_fusion.5
  103.3 1.9 %fusion.13 = f32[1024,512]{1,0:T(8,128)S(1)} fusion(bf16[1,1024,1024]{2,1,0:T(8,128)(2,1)S(1)} %get-tuple-element.8, s32[]{:T(128)S(6)} %select_n.122, bf16[512,1,512]{2,1,0:T(2,128)(2,1)} %get-tuple-element.15), kind=kOutput, calls=%fused_computation.18 | convolution fusion | flops 536870912 | bytes 3670020 | tf_op jit(solution)/shard_map/dot_general | solution.py:35
  105.2 13.1 %collective-permute-done.4 = bf16[512,512]{1,0:T(8,128)(2,1)S(1)} collective-permute-done((bf16[512,512]{1,0:T(8,128)(2,1)S(1)}, bf16[512,512]{1,0:T(8,128)(2,1)S(1)}, u32[]{:S(2)}, u32[]{:S(2)}) %collective-permute-start.4) | collective-permute-done | bytes 524320 | tf_op jit(solution)/shard_map/ppermute | solution.py:14
  118.3 0.7 select_convert_fusion
  119.0 0.1 constant_dynamic-slice_fusion.3
  119.1 0.1 pad_maximum_fusion
  119.2 1.6 %collective-permute-start.5 = (bf16[2,256,512]{2,1,0:T(8,128)(2,1)S(1)}, bf16[2,256,512]{2,1,0:T(8,128)(2,1)S(1)}, u32[]{:S(2)}, u32[]{:S(2)}) collective-permute-start(bf16[2,256,512]{2,1,0:T(8,128)(2,1)S(1)} %pad_maximum_fusion), channel_id=1, source_target_pairs={{0,2},{1,3},{2,0},{3,1},{4,6},{5,7},{6,4},{7,5},{8,10},{9,11},{10,... | collective-permute-start | bytes 1572872 | tf_op jit(solution)/shard_map/ppermute | solution.py:14
  120.7 12.2 %collective-permute-done.5 = bf16[2,256,512]{2,1,0:T(8,128)(2,1)S(1)} collective-permute-done((bf16[2,256,512]{2,1,0:T(8,128)(2,1)S(1)}, bf16[2,256,512]{2,1,0:T(8,128)(2,1)S(1)}, u32[]{:S(2)}, u32[]{:S(2)}) %collective-permute-start.5) | collective-permute-done | bytes 524320 | tf_op jit(solution)/shard_map/ppermute | solution.py:14
  133.0 0.2 convert_add_fusion
  133.2 0.1 collective-permute-start.6
  133.2 1.5 %collective-permute-done.6 = bf16[256,512]{1,0:T(8,128)(2,1)S(1)} collective-permute-done((bf16[256,512]{1,0:T(8,128)(2,1)S(1)}, bf16[256,512]{1,0:T(8,128)(2,1)S(1)}, u32[]{:S(2)}, u32[]{:S(2)}) %collective-permute-start.6) | collective-permute-done | bytes 262176 | tf_op jit(solution)/shard_map/ppermute | solution.py:14
  134.8 0.8 fusion.26
  (1 shorter events, 0.0 us)
Async XLA Ops:
  7.1 27.5 %collective-permute-start = (bf16[512,512]{1,0:T(8,128)(2,1)}, bf16[512,512]{1,0:T(8,128)(2,1)}, u32[]{:S(2)}, u32[]{:S(2)}) collective-permute-start(bf16[512,512]{1,0:T(8,128)(2,1)} %bitcast.83), channel_id=1, source_target_pairs={{0,8},{1,9},{2,10},{3,11},{4,12},{5,13},{6,14},{7,15},{8,0},{9,1},... | collective-permute-start | bytes 1572872 | tf_op jit(solution)/shard_map/ppermute | solution.py:14
  18.5 16.1 %copy-start.3 = (bf16[1,1024,1024]{2,1,0:T(8,128)(2,1)S(1)}, bf16[1,1024,1024]{2,1,0:T(8,128)(2,1)}, u32[]{:S(2)}) copy-start(bf16[1,1024,1024]{2,1,0:T(8,128)(2,1)} %get-tuple-element.5) | copy-start | bytes 6291460
  42.1 13.2 %collective-permute-start.1 = (bf16[512,512]{1,0:T(8,128)(2,1)S(1)}, bf16[512,512]{1,0:T(8,128)(2,1)S(1)}, u32[]{:S(2)}, u32[]{:S(2)}) collective-permute-start(bf16[512,512]{1,0:T(8,128)(2,1)S(1)} %bitcast.86), channel_id=1, source_target_pairs={{0,4},{1,5},{2,6},{3,7},{4,0},{5,1},{6,2},{7,3},{8,12},{9,13},{10,... | collective-permute-start | bytes 1572872 | tf_op jit(solution)/shard_map/ppermute | solution.py:14
  42.9 12.4 %copy-start.2 = (bf16[1,1024,1024]{2,1,0:T(8,128)(2,1)S(1)}, bf16[1,1024,1024]{2,1,0:T(8,128)(2,1)}, u32[]{:S(2)}) copy-start(bf16[1,1024,1024]{2,1,0:T(8,128)(2,1)} %get-tuple-element.9) | copy-start | bytes 6291460
  61.9 12.2 %collective-permute-start.2 = (bf16[512,512]{1,0:T(8,128)(2,1)S(1)}, bf16[512,512]{1,0:T(8,128)(2,1)S(1)}, u32[]{:S(2)}, u32[]{:S(2)}) collective-permute-start(bf16[512,512]{1,0:T(8,128)(2,1)S(1)} %bitcast.87), channel_id=1, source_target_pairs={{0,2},{1,3},{2,0},{3,1},{4,6},{5,7},{6,4},{7,5},{8,10},{9,11},{10,... | collective-permute-start | bytes 1572872 | tf_op jit(solution)/shard_map/ppermute | solution.py:14
  63.2 10.9 %copy-start.1 = (bf16[1,1024,1024]{2,1,0:T(8,128)(2,1)S(1)}, bf16[1,1024,1024]{2,1,0:T(8,128)(2,1)}, u32[]{:S(2)}) copy-start(bf16[1,1024,1024]{2,1,0:T(8,128)(2,1)} %get-tuple-element.6) | copy-start | bytes 6291460
  80.6 3.1 %collective-permute-start.3 = (bf16[512,512]{1,0:T(8,128)(2,1)S(1)}, bf16[512,512]{1,0:T(8,128)(2,1)S(1)}, u32[]{:S(2)}, u32[]{:S(2)}) collective-permute-start(bf16[512,512]{1,0:T(8,128)(2,1)S(1)} %bitcast.88), channel_id=1, source_target_pairs={{0,1},{1,0},{2,3},{3,2},{4,5},{5,4},{6,7},{7,6},{8,9},{9,8},{10,11... | collective-permute-start | bytes 1572872 | tf_op jit(solution)/shard_map/ppermute | solution.py:14
  80.7 3.0 %copy-start = (bf16[1,1024,1024]{2,1,0:T(8,128)(2,1)S(1)}, bf16[1,1024,1024]{2,1,0:T(8,128)(2,1)}, u32[]{:S(2)}) copy-start(bf16[1,1024,1024]{2,1,0:T(8,128)(2,1)} %get-tuple-element.7) | copy-start | bytes 6291460
  86.9 7.6 %copy-start.4 = (s32[16]{0:T(128)S(1)}, s32[16]{0:T(128)}, u32[]{:S(2)}) copy-start(s32[16]{0:T(128)} %param.7) | copy-start | bytes 196
  90.2 28.1 %collective-permute-start.4 = (bf16[512,512]{1,0:T(8,128)(2,1)S(1)}, bf16[512,512]{1,0:T(8,128)(2,1)S(1)}, u32[]{:S(2)}, u32[]{:S(2)}) collective-permute-start(bf16[512,512]{1,0:T(8,128)(2,1)S(1)} %bitcast.85), channel_id=1, source_target_pairs={{0,8},{1,9},{2,10},{3,11},{4,12},{5,13},{6,14},{7,15},{8,0},{9,1},... | collective-permute-start | bytes 1572872 | tf_op jit(solution)/shard_map/ppermute | solution.py:14
  119.2 13.8 %collective-permute-start.5 = (bf16[2,256,512]{2,1,0:T(8,128)(2,1)S(1)}, bf16[2,256,512]{2,1,0:T(8,128)(2,1)S(1)}, u32[]{:S(2)}, u32[]{:S(2)}) collective-permute-start(bf16[2,256,512]{2,1,0:T(8,128)(2,1)S(1)} %pad_maximum_fusion), channel_id=1, source_target_pairs={{0,2},{1,3},{2,0},{3,1},{4,6},{5,7},{6,4},{7,5},{8,10},{9,11},{10,... | collective-permute-start | bytes 1572872 | tf_op jit(solution)/shard_map/ppermute | solution.py:14
  133.2 1.6 %collective-permute-start.6 = (bf16[256,512]{1,0:T(8,128)(2,1)S(1)}, bf16[256,512]{1,0:T(8,128)(2,1)S(1)}, u32[]{:S(2)}, u32[]{:S(2)}) collective-permute-start(bf16[256,512]{1,0:T(8,128)(2,1)S(1)} %fusion.29), channel_id=1, source_target_pairs={{0,1},{1,0},{2,3},{3,2},{4,5},{5,4},{6,7},{7,6},{8,9},{9,8},{10,11... | collective-permute-start | bytes 786440 | tf_op jit(solution)/shard_map/ppermute | solution.py:14
where the time goes:
time: 136 us
  waiting for transfers between devices  57.5 us (42%)
  local copies, waits for them, and re-layouts  32.4 us (24%)
  matrix products  19.2 us (14%)
  starting transfers between devices  12.1 us (9%)
  between operations  7.7 us (6%)
  other arithmetic  6.6 us (5%)
    ppermute x7, waiting for transfers between devices, from_partner(): return lax.ppermute(value, axis, pairs)  57.5 us
    dynamic_slice x5, local copies, waits for them, and re-layouts, shards(): lax.dynamic_index_in_dim(paired_rows, 1 - which_half, 1, keepdims=False)  14.8 us
    ppermute x7, starting transfers between devices, from_partner(): return lax.ppermute(value, axis, pairs)  12.1 us
    dot_general x5, matrix products, shards(): product = jnp.dot(own_cols, own_half, preferred_element_type=jnp.float32)  10.7 us
    dot_general x5, matrix products, shards(): jnp.dot(peer_cols, received, preferred_element_type=jnp.float32)  8.59 us
    slice x1, local copies, waits for them, and re-layouts, shards(): matrix = transfer[level_idx]  7.41 us
    reshape x5, local copies, waits for them, and re-layouts, shards(): paired_rows = current.reshape(half_rows, 2, W)  6.48 us
    lt x5, other arithmetic, shards(): keep_rows = (row_ids < ranks[level_idx + 1, 0])[:, None]  3.64 us
  transfers between devices with their start and end apart: 7, of which 6 were waited for; matrix products, arithmetic and copies ran while one was open for 17% of the time, Pallas kernels for 0%

commit v1 on v0

v1 whole, which is shorter than its diff:
```python
import functools

import jax
import jax.numpy as jnp
from jax import lax
from jax.experimental import pallas as pl
from jax.experimental.pallas import tpu as pltpu
from jax.sharding import PartitionSpec as P

CHUNK = 128
TILES = 4
ANY = pl.BlockSpec(memory_space=pl.ANY)
VMEM = pl.BlockSpec(memory_space=pltpu.VMEM)
SMEM = pl.BlockSpec(memory_space=pltpu.SMEM)
PARAMS = pltpu.CompilerParams(vmem_limit_bytes=8 * 1024 * 1024)


def from_partner(value, axis, apart):
    mask = 2**apart
    pairs = [(source, source ^ mask) for source in range(lax.axis_size(axis))]
    return lax.ppermute(value, axis, pairs)


def bit_of(apart):
    return lax.axis_index("bfly") >> apart & 1


def split_rows(values, first_row, ranks, level, half, y, own, other, base):
    rows, width = values.shape
    ids = lax.broadcasted_iota(jnp.int32, (rows, width), 0) + first_row
    y[...] = jnp.where(ids < ranks[level], values, 0.0)
    out = pl.ds(base, rows // 2)
    own[out, :] = y[pl.ds(half, rows // 2, stride=2), :].astype(jnp.bfloat16)
    other[out, :] = y[pl.ds(1 - half, rows // 2, stride=2), :].astype(jnp.bfloat16)


def first_kernel(apart, ranks, x, own, other, y):
    rows = x.shape[0] // TILES
    half = bit_of(apart)
    for tile in range(TILES):
        values = x[pl.ds(tile * rows, rows), :].astype(jnp.float32)
        split_rows(values, tile * rows, ranks, 0, half, y.at[tile], own, other, tile * rows // 2)


def stack_halves(apart, own, received, z):
    half_rows = own.shape[0]
    half = bit_of(apart)
    z[pl.ds(pl.multiple_of(half * half_rows, half_rows), half_rows), :] = own[...]
    z[pl.ds(pl.multiple_of((1 - half) * half_rows, half_rows), half_rows), :] = received[...]


def level_kernel(level, apart, next_apart, ranks, transfer, own, received, next_own, next_other, z, y):
    stack_halves(apart, own, received, z)
    rows = transfer.shape[1] // TILES
    half = bit_of(next_apart)
    for tile in range(TILES):
        matrix = transfer[level, pl.ds(tile * rows, rows), :]
        values = jnp.dot(matrix, z[...], preferred_element_type=jnp.float32)
        split_rows(values, tile * rows, ranks, level + 1, half, y.at[tile], next_own, next_other, tile * rows // 2)


def last_kernel(level, apart, ranks, owners, transfer, own, received, kept, sent, z, x):
    stack_halves(apart, own, received, z)
    rows = transfer.shape[1] // 4
    for tile in range(4):
        matrix = transfer[level, pl.ds(tile * rows, rows), :]
        values = jnp.dot(matrix, z[...], preferred_element_type=jnp.float32)
        ids = lax.broadcasted_iota(jnp.int32, values.shape, 0) + tile * rows
        x[pl.ds(tile * rows, rows), :] = jnp.where(ids < ranks[level + 1], values, 0.0).astype(jnp.bfloat16)
    position = lax.axis_index("bfly")
    for target, slot, flip in ((kept, 0, 0), (kept, 1, 2), (sent, 0, 1), (sent, 1, 3)):
        quarter = owners[position ^ flip]
        target[slot] = x[pl.ds(pl.multiple_of(quarter * rows, rows), rows), :]


def shape(*dims):
    return jax.ShapeDtypeStruct(dims, jnp.bfloat16)


def shards(coefficients, transfer, ranks, owner_map):
    rows, width = coefficients.shape
    levels = transfer.shape[0]
    ranks = ranks.reshape(-1)
    half, quarter = rows // 2, rows // 4
    count = lax.axis_size("bfly")
    log_count = count.bit_length() - 1
    bits = [(log_count - 1 - level) % log_count for level in range(levels)]
    tiles = pltpu.VMEM((TILES, rows // TILES, CHUNK), jnp.float32)
    stacked = pltpu.VMEM((rows, CHUNK), jnp.bfloat16)
    kept_all, sums = [], []

    for chunk in range(width // CHUNK):
        own, other = pl.pallas_call(
            functools.partial(first_kernel, bits[0]),
            out_shape=[shape(half, CHUNK)] * 2,
            grid=(1,),
            in_specs=[SMEM, pl.BlockSpec((rows, CHUNK), functools.partial(lambda c, i: (0, c), chunk))],
            out_specs=[pl.BlockSpec((half, CHUNK), lambda i: (0, 0))] * 2,
            scratch_shapes=[tiles],
            compiler_params=PARAMS,
        )(ranks, coefficients)
        for level in range(levels):
            received = from_partner(other, "bfly", bits[level])
            cost = pl.CostEstimate(flops=2 * rows * rows * CHUNK, bytes_accessed=rows * rows * 2, transcendentals=0)
            if level + 1 < levels:
                own, other = pl.pallas_call(
                    functools.partial(level_kernel, level, bits[level], bits[level + 1]),
                    out_shape=[shape(half, CHUNK)] * 2,
                    in_specs=[SMEM, VMEM, VMEM, VMEM],
                    out_specs=[VMEM, VMEM],
                    scratch_shapes=[stacked, tiles],
                    cost_estimate=cost,
                    compiler_params=PARAMS,
                )(ranks, transfer, own, received)
            else:
                kept, sent = pl.pallas_call(
                    functools.partial(last_kernel, level, bits[level]),
                    out_shape=[shape(2, quarter, CHUNK)] * 2,
                    in_specs=[SMEM, SMEM, VMEM, VMEM, VMEM],
                    out_specs=[VMEM, VMEM],
                    scratch_shapes=[stacked, stacked],
                    cost_estimate=cost,
                    compiler_params=PARAMS,
                )(ranks, owner_map, transfer, own, received)
        arrived = from_partner(sent, "bfly", 0)
        partial_sum = kept.astype(jnp.float32) + arrived.astype(jnp.float32)
        far_sum = from_partner(partial_sum[1].astype(jnp.bfloat16), "bfly", 1)
        sums.append((partial_sum[0] + far_sum.astype(jnp.float32)).astype(jnp.bfloat16))
    return jnp.concatenate(sums, axis=1)


def solution(mesh):
    in_specs = (P(("freq", "bfly"), None), P(None, ("freq", "bfly"), None), P(None, "bfly"), P())
    out_specs = P(("freq", "bfly"), None)
    return jax.shard_map(shards, mesh=mesh, in_specs=in_specs, out_specs=out_specs, check_vma=False)
```

time: 136 us -> 92.4 us (0.68)
  waiting for transfers between devices: 57.5 us -> 27 us
  Pallas kernels: 0 us -> 29.2 us
  local copies, waits for them, and re-layouts: 32.4 us -> 8.5 us
  matrix products: 19.2 us -> 0 us
  starting transfers between devices: 12.1 us -> 26.2 us
  between operations: 7.7 us -> 0.31 us
  other arithmetic: 6.6 us -> 0.92 us
    ppermute x7 -> x28, waiting for transfers between devices: 57.5 us -> 27 us  [from_partner(): return lax.ppermute(value, axis, pairs)]
    pallas_call x0 -> x24, Pallas kernels: none -> 29.2 us  [the longest x16 21.4 us: shards(): pl.pallas_call(functools.partial(level_kernel, level, bits[level], bits[l...]
    dot_general x10 -> x0, matrix products: 19.2 us -> none  [the longest x5 10.7 us: shards(): product = jnp.dot(own_cols, own_half, preferred_element_type=jnp.float32)]
    dynamic_slice x7 -> x0, local copies, waits for them, and re-layouts: 15.5 us -> none  [the longest x5 14.8 us: shards(): lax.dynamic_index_in_dim(paired_rows, 1 - which_half, 1, keepdims=False)]
    ppermute x7 -> x28, starting transfers between devices: 12.1 us -> 26.2 us  [from_partner(): return lax.ppermute(value, axis, pairs)]
    slice x2 -> x0, local copies, waits for them, and re-layouts: 8.91 us -> none  [the longest x1 7.41 us: shards(): matrix = transfer[level_idx]]
    unnamed x15 -> x10, local copies, waits for them, and re-layouts: 1.45 us -> 8.46 us
    reshape x5 -> x0, local copies, waits for them, and re-layouts: 6.48 us -> none  [shards(): paired_rows = current.reshape(half_rows, 2, W)]
  transfers between devices with their start and end apart: 7 -> 28, of which waited for: 6 -> 10; matrix products, arithmetic and copies ran while one was open for 17% -> 0% of each run, Pallas kernels for 0% -> 31%
where the time goes in v1:
time: 92.4 us; the launch traced here: 92.2 us
  Pallas kernels  29.2 us (32%)
  waiting for transfers between devices  27 us (29%)
  starting transfers between devices  26.2 us (28%)
  local copies, waits for them, and re-layouts  8.5 us (9%)
    ppermute x28, waiting for transfers between devices, from_partner(): return lax.ppermute(value, axis, pairs)  27 us
    ppermute x28, starting transfers between devices, from_partner(): return lax.ppermute(value, axis, pairs)  26.2 us
    pallas_call x16, Pallas kernels, shards(): pl.pallas_call(functools.partial(level_kernel, level, bits[level], bits[l...  21.4 us
    unnamed x10, local copies, waits for them, and re-layouts  8.46 us
    pallas_call x4, Pallas kernels, shards(): pl.pallas_call(functools.partial(last_kernel, level, bits[level]), out_sh...  5.14 us
    pallas_call x4, Pallas kernels, shards(): pl.pallas_call(functools.partial(first_kernel, bits[0]), out_shape=[shape...  2.65 us
  transfers between devices with their start and end apart: 28, of which 10 were waited for; matrix products, arithmetic and copies ran while one was open for 0% of the time, Pallas kernels for 31%

profile of v1, /device:TPU:0, one launch (start us, length us, event | category | flops | bytes accessed | tf_op | source)
XLA Modules:
  0.0 92.2 jit_solution(15949138446510511027)
XLA Ops:
  0.0 1.2 %copy-done.2 = bf16[1024,512]{1,0:T(8,128)(2,1)S(1)} copy-done((bf16[1024,512]{1,0:T(8,128)(2,1)S(1)}, bf16[1024,512]{1,0:T(8,128)(2,1)}, u32[]{:S(2)}) %copy-start.2) | copy-done | bytes 1048600
  1.2 0.7 copy-done.3
  1.9 0.7 shard_map.64
  2.6 4.1 %collective-permute-start.21 = (bf16[512,128]{1,0:T(8,128)(2,1)S(1)}, bf16[512,128]{1,0:T(8,128)(2,1)S(1)}, u32[]{:S(2)}, u32[]{:S(2)}) collective-permute-start(bf16[512,128]{1,0:T(8,128)(2,1)S(1)} %get-tuple-element.90), channel_id=1, source_target_pairs={{0,8},{1,9},{2,10},{3,11},{4,12},{5,13},{6,14},{7,15},{8,0},{9,1},... | collective-permute-start | bytes 393224 | tf_op jit(solution)/shard_map/ppermute | solution.py:21
  6.7 0.7 shard_map.58
  7.3 0.1 collective-permute-start.14
  7.4 0.7 shard_map.52
  8.1 3.0 %collective-permute-start.7 = (bf16[512,128]{1,0:T(8,128)(2,1)S(1)}, bf16[512,128]{1,0:T(8,128)(2,1)S(1)}, u32[]{:S(2)}, u32[]{:S(2)}) collective-permute-start(bf16[512,128]{1,0:T(8,128)(2,1)S(1)} %get-tuple-element.66), channel_id=1, source_target_pairs={{0,8},{1,9},{2,10},{3,11},{4,12},{5,13},{6,14},{7,15},{8,0},{9,1},... | collective-permute-start | bytes 393224 | tf_op jit(solution)/shard_map/ppermute | solution.py:21
  11.0 0.7 shard_map.46
  11.7 0.1 collective-permute-start
  11.8 10.4 %collective-permute-done.21.received = bf16[512,128]{1,0:T(8,128)(2,1)S(1)} collective-permute-done((bf16[512,128]{1,0:T(8,128)(2,1)S(1)}, bf16[512,128]{1,0:T(8,128)(2,1)S(1)}, u32[]{:S(2)}, u32[]{:S(2)}) %collective-permute-start.21) | collective-permute-done | bytes 131104 | tf_op jit(solution)/shard_map/ppermute | solution.py:21
  22.2 4.0 %copy-done = bf16[5,1024,1024]{2,1,0:T(8,128)(2,1)S(1)} copy-done((bf16[5,1024,1024]{2,1,0:T(8,128)(2,1)S(1)}, bf16[5,1024,1024]{2,1,0:T(8,128)(2,1)}, u32[]{:S(2)}) %copy-start) | copy-done | bytes 10485784
  26.2 1.3 %shard_map.65 = (bf16[512,128]{1,0:T(8,128)(2,1)S(1)}, bf16[512,128]{1,0:T(8,128)(2,1)S(1)}) custom-call(s32[6]{0:T(128)S(1)} %bitcast.37, bf16[5,1024,1024]{2,1,0:T(8,128)(2,1)S(1)} %copy-done, bf16[512,128]{1,0:T(8,128)(2,1)S(1)} %get-tuple-element.89.own, bf16[512,128]{1,0:T(8,128)(2,1)S(1)} %collective-permute-done.21.received), custom_call_target="tpu_custom_call" | custom-call | flops 268435456 | bytes 2097152 | tf_op jit(solution)/shard_map/pallas_call | solution.py:106
  27.6 2.6 %copy-done.1 = bf16[5,1024,1024]{2,1,0:T(8,128)(2,1)S(1)} copy-done((bf16[5,1024,1024]{2,1,0:T(8,128)(2,1)S(1)}, bf16[5,1024,1024]{2,1,0:T(8,128)(2,1)}, u32[]{:S(2)}) %copy-start.1) | copy-done | bytes 10485784
  30.2 1.3 %shard_map.59 = (bf16[512,128]{1,0:T(8,128)(2,1)S(1)}, bf16[512,128]{1,0:T(8,128)(2,1)S(1)}) custom-call(s32[6]{0:T(128)S(1)} %bitcast.38, bf16[5,1024,1024]{2,1,0:T(8,128)(2,1)S(1)} %copy-done.1, bf16[512,128]{1,0:T(8,128)(2,1)S(1)} %get-tuple-element.77.own, bf16[512,128]{1,0:T(8,128)(2,1)S(1)} %collective-permute-done.14.received), custom_call_target="tpu_custom_call" | custom-call | flops 268435456 | bytes 2097152 | tf_op jit(solution)/shard_map/pallas_call | solution.py:106
  31.5 0.1 collective-permute-start.15
  31.6 1.3 %shard_map.53 = (bf16[512,128]{1,0:T(8,128)(2,1)S(1)}, bf16[512,128]{1,0:T(8,128)(2,1)S(1)}) custom-call(s32[6]{0:T(128)S(1)} %bitcast.39, bf16[5,1024,1024]{2,1,0:T(8,128)(2,1)S(1)} %copy-done.1, bf16[512,128]{1,0:T(8,128)(2,1)S(1)} %get-tuple-element.65.own, bf16[512,128]{1,0:T(8,128)(2,1)S(1)} %collective-permute-done.7.received), custom_call_target="tpu_custom_call" | custom-call | flops 268435456 | bytes 2097152 | tf_op jit(solution)/shard_map/pallas_call | solution.py:106
  33.0 2.1 %collective-permute-start.8 = (bf16[512,128]{1,0:T(8,128)(2,1)S(1)}, bf16[512,128]{1,0:T(8,128)(2,1)S(1)}, u32[]{:S(2)}, u32[]{:S(2)}) collective-permute-start(bf16[512,128]{1,0:T(8,128)(2,1)S(1)} %get-tuple-element.68), channel_id=1, source_target_pairs={{0,4},{1,5},{2,6},{3,7},{4,0},{5,1},{6,2},{7,3},{8,12},{9,13},{10,... | collective-permute-start | bytes 393224 | tf_op jit(solution)/shard_map/ppermute | solution.py:21
  35.0 1.3 %shard_map.47 = (bf16[512,128]{1,0:T(8,128)(2,1)S(1)}, bf16[512,128]{1,0:T(8,128)(2,1)S(1)}) custom-call(s32[6]{0:T(128)S(1)} %bitcast.40, bf16[5,1024,1024]{2,1,0:T(8,128)(2,1)S(1)} %copy-done.1, bf16[512,128]{1,0:T(8,128)(2,1)S(1)} %get-tuple-element.53.own, bf16[512,128]{1,0:T(8,128)(2,1)S(1)} %collective-permute-done.received), custom_call_target="tpu_custom_call" | custom-call | flops 268435456 | bytes 2097152 | tf_op jit(solution)/shard_map/pallas_call | solution.py:106
  36.4 0.1 collective-permute-start.1
  36.5 1.3 %shard_map.66 = (bf16[512,128]{1,0:T(8,128)(2,1)S(1)}, bf16[512,128]{1,0:T(8,128)(2,1)S(1)}) custom-call(s32[6]{0:T(128)S(1)} %bitcast.41, bf16[5,1024,1024]{2,1,0:T(8,128)(2,1)S(1)} %copy-done.1, bf16[512,128]{1,0:T(8,128)(2,1)S(1)} %get-tuple-element.91.own, bf16[512,128]{1,0:T(8,128)(2,1)S(1)} %collective-permute-done.22.received), custom_call_target="tpu_custom_call" | custom-call | flops 268435456 | bytes 2097152 | tf_op jit(solution)/shard_map/pallas_call | solution.py:106
  37.8 1.9 %collective-permute-start.23 = (bf16[512,128]{1,0:T(8,128)(2,1)S(1)}, bf16[512,128]{1,0:T(8,128)(2,1)S(1)}, u32[]{:S(2)}, u32[]{:S(2)}) collective-permute-start(bf16[512,128]{1,0:T(8,128)(2,1)S(1)} %get-tuple-element.94), channel_id=1, source_target_pairs={{0,2},{1,3},{2,0},{3,1},{4,6},{5,7},{6,4},{7,5},{8,10},{9,11},{10,... | collective-permute-start | bytes 393224 | tf_op jit(solution)/shard_map/ppermute | solution.py:21
  39.7 1.3 %shard_map.60 = (bf16[512,128]{1,0:T(8,128)(2,1)S(1)}, bf16[512,128]{1,0:T(8,128)(2,1)S(1)}) custom-call(s32[6]{0:T(128)S(1)} %bitcast.42, bf16[5,1024,1024]{2,1,0:T(8,128)(2,1)S(1)} %copy-done.1, bf16[512,128]{1,0:T(8,128)(2,1)S(1)} %get-tuple-element.79.own, bf16[512,128]{1,0:T(8,128)(2,1)S(1)} %collective-permute-done.15.received), custom_call_target="tpu_custom_call" | custom-call | flops 268435456 | bytes 2097152 | tf_op jit(solution)/shard_map/pallas_call | solution.py:106
  41.0 0.3 collective-permute-start.16
  41.3 1.3 %shard_map.54 = (bf16[512,128]{1,0:T(8,128)(2,1)S(1)}, bf16[512,128]{1,0:T(8,128)(2,1)S(1)}) custom-call(s32[6]{0:T(128)S(1)} %bitcast.43, bf16[5,1024,1024]{2,1,0:T(8,128)(2,1)S(1)} %copy-done.1, bf16[512,128]{1,0:T(8,128)(2,1)S(1)} %get-tuple-element.67.own, bf16[512,128]{1,0:T(8,128)(2,1)S(1)} %collective-permute-done.8.received), custom_call_target="tpu_custom_call" | custom-call | flops 268435456 | bytes 2097152 | tf_op jit(solution)/shard_map/pallas_call | solution.py:106
  42.6 1.9 %collective-permute-start.9 = (bf16[512,128]{1,0:T(8,128)(2,1)S(1)}, bf16[512,128]{1,0:T(8,128)(2,1)S(1)}, u32[]{:S(2)}, u32[]{:S(2)}) collective-permute-start(bf16[512,128]{1,0:T(8,128)(2,1)S(1)} %get-tuple-element.70), channel_id=1, source_target_pairs={{0,2},{1,3},{2,0},{3,1},{4,6},{5,7},{6,4},{7,5},{8,10},{9,11},{10,... | collective-permute-start | bytes 393224 | tf_op jit(solution)/shard_map/ppermute | solution.py:21
  44.5 1.3 %shard_map.48 = (bf16[512,128]{1,0:T(8,128)(2,1)S(1)}, bf16[512,128]{1,0:T(8,128)(2,1)S(1)}) custom-call(s32[6]{0:T(128)S(1)} %bitcast.44, bf16[5,1024,1024]{2,1,0:T(8,128)(2,1)S(1)} %copy-done.1, bf16[512,128]{1,0:T(8,128)(2,1)S(1)} %get-tuple-element.55.own, bf16[512,128]{1,0:T(8,128)(2,1)S(1)} %collective-permute-done.1.received), custom_call_target="tpu_custom_call" | custom-call | flops 268435456 | bytes 2097152 | tf_op jit(solution)/shard_map/pallas_call | solution.py:106
  45.8 0.3 collective-permute-start.2
  46.1 1.3 %shard_map.67 = (bf16[512,128]{1,0:T(8,128)(2,1)S(1)}, bf16[512,128]{1,0:T(8,128)(2,1)S(1)}) custom-call(s32[6]{0:T(128)S(1)} %bitcast.45, bf16[5,1024,1024]{2,1,0:T(8,128)(2,1)S(1)} %copy-done.1, bf16[512,128]{1,0:T(8,128)(2,1)S(1)} %get-tuple-element.93.own, bf16[512,128]{1,0:T(8,128)(2,1)S(1)} %collective-permute-done.23.received), custom_call_target="tpu_custom_call" | custom-call | flops 268435456 | bytes 2097152 | tf_op jit(solution)/shard_map/pallas_call | solution.py:106
  47.4 0.1 collective-permute-start.24
  47.5 1.3 %shard_map.61 = (bf16[512,128]{1,0:T(8,128)(2,1)S(1)}, bf16[512,128]{1,0:T(8,128)(2,1)S(1)}) custom-call(s32[6]{0:T(128)S(1)} %bitcast.46, bf16[5,1024,1024]{2,1,0:T(8,128)(2,1)S(1)} %copy-done.1, bf16[512,128]{1,0:T(8,128)(2,1)S(1)} %get-tuple-element.81.own, bf16[512,128]{1,0:T(8,128)(2,1)S(1)} %collective-permute-done.16.received), custom_call_target="tpu_custom_call" | custom-call | flops 268435456 | bytes 2097152 | tf_op jit(solution)/shard_map/pallas_call | solution.py:106
  48.9 0.6 collective-permute-start.17
  49.4 0.4 collective-permute-done.9.received
  49.8 1.3 %shard_map.55 = (bf16[512,128]{1,0:T(8,128)(2,1)S(1)}, bf16[512,128]{1,0:T(8,128)(2,1)S(1)}) custom-call(s32[6]{0:T(128)S(1)} %bitcast.47, bf16[5,1024,1024]{2,1,0:T(8,128)(2,1)S(1)} %copy-done.1, bf16[512,128]{1,0:T(8,128)(2,1)S(1)} %get-tuple-element.69.own, bf16[512,128]{1,0:T(8,128)(2,1)S(1)} %collective-permute-done.9.received), custom_call_target="tpu_custom_call" | custom-call | flops 268435456 | bytes 2097152 | tf_op jit(solution)/shard_map/pallas_call | solution.py:106
  51.2 0.1 collective-permute-start.10
  51.3 1.3 %shard_map.49 = (bf16[512,128]{1,0:T(8,128)(2,1)S(1)}, bf16[512,128]{1,0:T(8,128)(2,1)S(1)}) custom-call(s32[6]{0:T(128)S(1)} %bitcast.48, bf16[5,1024,1024]{2,1,0:T(8,128)(2,1)S(1)} %copy-done.1, bf16[512,128]{1,0:T(8,128)(2,1)S(1)} %get-tuple-element.57.own, bf16[512,128]{1,0:T(8,128)(2,1)S(1)} %collective-permute-done.2.received), custom_call_target="tpu_custom_call" | custom-call | flops 268435456 | bytes 2097152 | tf_op jit(solution)/shard_map/pallas_call | solution.py:106
  52.6 0.6 collective-permute-start.3
  53.2 1.3 %shard_map.68 = (bf16[512,128]{1,0:T(8,128)(2,1)S(1)}, bf16[512,128]{1,0:T(8,128)(2,1)S(1)}) custom-call(s32[6]{0:T(128)S(1)} %bitcast.49, bf16[5,1024,1024]{2,1,0:T(8,128)(2,1)S(1)} %copy-done.1, bf16[512,128]{1,0:T(8,128)(2,1)S(1)} %get-tuple-element.95.own, bf16[512,128]{1,0:T(8,128)(2,1)S(1)} %collective-permute-done.24.received), custom_call_target="tpu_custom_call" | custom-call | flops 268435456 | bytes 2097152 | tf_op jit(solution)/shard_map/pallas_call | solution.py:106
  54.5 3.4 %collective-permute-start.25 = (bf16[512,128]{1,0:T(8,128)(2,1)S(1)}, bf16[512,128]{1,0:T(8,128)(2,1)S(1)}, u32[]{:S(2)}, u32[]{:S(2)}) collective-permute-start(bf16[512,128]{1,0:T(8,128)(2,1)S(1)} %get-tuple-element.98), channel_id=1, source_target_pairs={{0,8},{1,9},{2,10},{3,11},{4,12},{5,13},{6,14},{7,15},{8,0},{9,1},... | collective-permute-start | bytes 393224 | tf_op jit(solution)/shard_map/ppermute | solution.py:21
  57.9 1.3 %shard_map.62 = (bf16[512,128]{1,0:T(8,128)(2,1)S(1)}, bf16[512,128]{1,0:T(8,128)(2,1)S(1)}) custom-call(s32[6]{0:T(128)S(1)} %bitcast.50, bf16[5,1024,1024]{2,1,0:T(8,128)(2,1)S(1)} %copy-done.1, bf16[512,128]{1,0:T(8,128)(2,1)S(1)} %get-tuple-element.83.own, bf16[512,128]{1,0:T(8,128)(2,1)S(1)} %collective-permute-done.17.received), custom_call_target="tpu_custom_call" | custom-call | flops 268435456 | bytes 2097152 | tf_op jit(solution)/shard_map/pallas_call | solution.py:106
  59.2 0.1 collective-permute-start.18
  59.3 1.5 %shard_map.56 = (bf16[512,128]{1,0:T(8,128)(2,1)S(1)}, bf16[512,128]{1,0:T(8,128)(2,1)S(1)}) custom-call(s32[6]{0:T(128)S(1)} %bitcast.51, bf16[5,1024,1024]{2,1,0:T(8,128)(2,1)S(1)} %copy-done.1, bf16[512,128]{1,0:T(8,128)(2,1)S(1)} %get-tuple-element.71.own, bf16[512,128]{1,0:T(8,128)(2,1)S(1)} %collective-permute-done.10.received), custom_call_target="tpu_custom_call" | custom-call | flops 268435456 | bytes 2097152 | tf_op jit(solution)/shard_map/pallas_call | solution.py:106
  60.8 3.0 %collective-permute-start.11 = (bf16[512,128]{1,0:T(8,128)(2,1)S(1)}, bf16[512,128]{1,0:T(8,128)(2,1)S(1)}, u32[]{:S(2)}, u32[]{:S(2)}) collective-permute-start(bf16[512,128]{1,0:T(8,128)(2,1)S(1)} %get-tuple-element.74), channel_id=1, source_target_pairs={{0,8},{1,9},{2,10},{3,11},{4,12},{5,13},{6,14},{7,15},{8,0},{9,1},... | collective-permute-start | bytes 393224 | tf_op jit(solution)/shard_map/ppermute | solution.py:21
  63.8 1.3 %shard_map.50 = (bf16[512,128]{1,0:T(8,128)(2,1)S(1)}, bf16[512,128]{1,0:T(8,128)(2,1)S(1)}) custom-call(s32[6]{0:T(128)S(1)} %bitcast.52, bf16[5,1024,1024]{2,1,0:T(8,128)(2,1)S(1)} %copy-done.1, bf16[512,128]{1,0:T(8,128)(2,1)S(1)} %get-tuple-element.59.own, bf16[512,128]{1,0:T(8,128)(2,1)S(1)} %collective-permute-done.3.received), custom_call_target="tpu_custom_call" | custom-call | flops 268435456 | bytes 2097152 | tf_op jit(solution)/shard_map/pallas_call | solution.py:106
  65.1 0.1 collective-permute-start.4
  65.2 8.0 %collective-permute-done.25.received = bf16[512,128]{1,0:T(8,128)(2,1)S(1)} collective-permute-done((bf16[512,128]{1,0:T(8,128)(2,1)S(1)}, bf16[512,128]{1,0:T(8,128)(2,1)S(1)}, u32[]{:S(2)}, u32[]{:S(2)}) %collective-permute-start.25) | collective-permute-done | bytes 131104 | tf_op jit(solution)/shard_map/ppermute | solution.py:21
  73.2 1.3 %shard_map.69 = (bf16[2,256,128]{2,1,0:T(8,128)(2,1)S(1)}, bf16[2,256,128]{2,1,0:T(8,128)(2,1)S(1)}) custom-call(s32[6]{0:T(128)S(1)} %bitcast.53, s32[16]{0:T(128)S(1)} %copy-done.4, bf16[5,1024,1024]{2,1,0:T(8,128)(2,1)S(1)} %copy-done.1, bf16[512,128]{1,0:T(8,128)(2,1)S(1)} %get-tuple-element.97.own, bf16[512,128]{1,0:T(8,128)(2,1)S(1)} %collective-permute-done.25.received), custom_call_target="tpu_custom_call" | custom-call | flops 268435456 | bytes 2097152 | tf_op jit(solution)/shard_map/pallas_call | solution.py:116
  74.6 1.4 %collective-permute-done.18.received = bf16[512,128]{1,0:T(8,128)(2,1)S(1)} collective-permute-done((bf16[512,128]{1,0:T(8,128)(2,1)S(1)}, bf16[512,128]{1,0:T(8,128)(2,1)S(1)}, u32[]{:S(2)}, u32[]{:S(2)}) %collective-permute-start.18) | collective-permute-done | bytes 131104 | tf_op jit(solution)/shard_map/ppermute | solution.py:21
  76.0 1.3 %shard_map.63 = (bf16[2,256,128]{2,1,0:T(8,128)(2,1)S(1)}, bf16[2,256,128]{2,1,0:T(8,128)(2,1)S(1)}) custom-call(s32[6]{0:T(128)S(1)} %bitcast.54, s32[16]{0:T(128)S(1)} %copy-done.4, bf16[5,1024,1024]{2,1,0:T(8,128)(2,1)S(1)} %copy-done.1, bf16[512,128]{1,0:T(8,128)(2,1)S(1)} %get-tuple-element.85.own, bf16[512,128]{1,0:T(8,128)(2,1)S(1)} %collective-permute-done.18.received), custom_call_target="tpu_custom_call" | custom-call | flops 268435456 | bytes 2097152 | tf_op jit(solution)/shard_map/pallas_call | solution.py:116
  77.3 0.1 collective-permute-start.19
  77.4 1.4 %collective-permute-done.11.received = bf16[512,128]{1,0:T(8,128)(2,1)S(1)} collective-permute-done((bf16[512,128]{1,0:T(8,128)(2,1)S(1)}, bf16[512,128]{1,0:T(8,128)(2,1)S(1)}, u32[]{:S(2)}, u32[]{:S(2)}) %collective-permute-start.11) | collective-permute-done | bytes 131104 | tf_op jit(solution)/shard_map/ppermute | solution.py:21
  78.8 1.3 %shard_map.57 = (bf16[2,256,128]{2,1,0:T(8,128)(2,1)S(1)}, bf16[2,256,128]{2,1,0:T(8,128)(2,1)S(1)}) custom-call(s32[6]{0:T(128)S(1)} %bitcast.55, s32[16]{0:T(128)S(1)} %copy-done.4, bf16[5,1024,1024]{2,1,0:T(8,128)(2,1)S(1)} %copy-done.1, bf16[512,128]{1,0:T(8,128)(2,1)S(1)} %get-tuple-element.73.own, bf16[512,128]{1,0:T(8,128)(2,1)S(1)} %collective-permute-done.11.received), custom_call_target="tpu_custom_call" | custom-call | flops 268435456 | bytes 2097152 | tf_op jit(solution)/shard_map/pallas_call | solution.py:116
  80.1 0.1 collective-permute-start.12
  80.2 1.0 %collective-permute-done.4.received = bf16[512,128]{1,0:T(8,128)(2,1)S(1)} collective-permute-done((bf16[512,128]{1,0:T(8,128)(2,1)S(1)}, bf16[512,128]{1,0:T(8,128)(2,1)S(1)}, u32[]{:S(2)}, u32[]{:S(2)}) %collective-permute-start.4) | collective-permute-done | bytes 131104 | tf_op jit(solution)/shard_map/ppermute | solution.py:21
  81.2 1.3 %shard_map.51 = (bf16[2,256,128]{2,1,0:T(8,128)(2,1)S(1)}, bf16[2,256,128]{2,1,0:T(8,128)(2,1)S(1)}) custom-call(s32[6]{0:T(128)S(1)} %bitcast.56, s32[16]{0:T(128)S(1)} %copy-done.4, bf16[5,1024,1024]{2,1,0:T(8,128)(2,1)S(1)} %copy-done.1, bf16[512,128]{1,0:T(8,128)(2,1)S(1)} %get-tuple-element.61.own, bf16[512,128]{1,0:T(8,128)(2,1)S(1)} %collective-permute-done.4.received), custom_call_target="tpu_custom_call" | custom-call | flops 268435456 | bytes 2097152 | tf_op jit(solution)/shard_map/pallas_call | solution.py:116
  82.7 1.3 %collective-permute-start.27 = (bf16[256,128]{1,0:T(8,128)(2,1)S(1)}, bf16[256,128]{1,0:T(8,128)(2,1)S(1)}, u32[]{:S(2)}, u32[]{:S(2)}) collective-permute-start(bf16[256,128]{1,0:T(8,128)(2,1)S(1)} %fusion.11), channel_id=1, source_target_pairs={{0,2},{1,3},{2,0},{3,1},{4,6},{5,7},{6,4},{7,5},{8,10},{9,11},{10,... | collective-permute-start | bytes 196616 | tf_op jit(solution)/shard_map/ppermute | solution.py:21
  84.1 0.8 collective-permute-start.20
  84.9 1.3 %collective-permute-start.13 = (bf16[256,128]{1,0:T(8,128)(2,1)S(1)}, bf16[256,128]{1,0:T(8,128)(2,1)S(1)}, u32[]{:S(2)}, u32[]{:S(2)}) collective-permute-start(bf16[256,128]{1,0:T(8,128)(2,1)S(1)} %fusion.9), channel_id=1, source_target_pairs={{0,2},{1,3},{2,0},{3,1},{4,6},{5,7},{6,4},{7,5},{8,10},{9,11},{10,... | collective-permute-start | bytes 196616 | tf_op jit(solution)/shard_map/ppermute | solution.py:21
  86.3 0.8 collective-permute-start.6
  87.2 0.4 collective-permute-done.27
  87.6 1.5 %collective-permute-done.20 = bf16[256,128]{1,0:T(8,128)(2,1)S(1)} collective-permute-done((bf16[256,128]{1,0:T(8,128)(2,1)S(1)}, bf16[256,128]{1,0:T(8,128)(2,1)S(1)}, u32[]{:S(2)}, u32[]{:S(2)}) %collective-permute-start.20) | collective-permute-done | bytes 65568 | tf_op jit(solution)/shard_map/ppermute | solution.py:21
  89.1 1.4 %collective-permute-done.13 = bf16[256,128]{1,0:T(8,128)(2,1)S(1)} collective-permute-done((bf16[256,128]{1,0:T(8,128)(2,1)S(1)}, bf16[256,128]{1,0:T(8,128)(2,1)S(1)}, u32[]{:S(2)}, u32[]{:S(2)}) %collective-permute-start.13) | collective-permute-done | bytes 65568 | tf_op jit(solution)/shard_map/ppermute | solution.py:21
  90.5 1.0 %collective-permute-done.6 = bf16[256,128]{1,0:T(8,128)(2,1)S(1)} collective-permute-done((bf16[256,128]{1,0:T(8,128)(2,1)S(1)}, bf16[256,128]{1,0:T(8,128)(2,1)S(1)}, u32[]{:S(2)}, u32[]{:S(2)}) %collective-permute-start.6) | collective-permute-done | bytes 65568 | tf_op jit(solution)/shard_map/ppermute | solution.py:21
  91.5 0.7 pad_maximum_fusion
  (39 shorter events, 0.5 us)
Async XLA Ops:
  0.0 1.2 %copy-start.2 = (bf16[1024,512]{1,0:T(8,128)(2,1)S(1)}, bf16[1024,512]{1,0:T(8,128)(2,1)}, u32[]{:S(2)}) copy-start(bf16[1024,512]{1,0:T(8,128)(2,1)} %x.7) | copy-start | bytes 3145732
  1.2 0.7 copy-start.3
  2.6 19.7 %collective-permute-start.21 = (bf16[512,128]{1,0:T(8,128)(2,1)S(1)}, bf16[512,128]{1,0:T(8,128)(2,1)S(1)}, u32[]{:S(2)}, u32[]{:S(2)}) collective-permute-start(bf16[512,128]{1,0:T(8,128)(2,1)S(1)} %get-tuple-element.90), channel_id=1, source_target_pairs={{0,8},{1,9},{2,10},{3,11},{4,12},{5,13},{6,14},{7,15},{8,0},{9,1},... | collective-permute-start | bytes 393224 | tf_op jit(solution)/shard_map/ppermute | solution.py:21
  7.3 20.3 %collective-permute-start.14 = (bf16[512,128]{1,0:T(8,128)(2,1)S(1)}, bf16[512,128]{1,0:T(8,128)(2,1)S(1)}, u32[]{:S(2)}, u32[]{:S(2)}) collective-permute-start(bf16[512,128]{1,0:T(8,128)(2,1)S(1)} %get-tuple-element.78), channel_id=1, source_target_pairs={{0,8},{1,9},{2,10},{3,11},{4,12},{5,13},{6,14},{7,15},{8,0},{9,1},... | collective-permute-start | bytes 393224 | tf_op jit(solution)/shard_map/ppermute | solution.py:21
  8.1 23.5 %collective-permute-start.7 = (bf16[512,128]{1,0:T(8,128)(2,1)S(1)}, bf16[512,128]{1,0:T(8,128)(2,1)S(1)}, u32[]{:S(2)}, u32[]{:S(2)}) collective-permute-start(bf16[512,128]{1,0:T(8,128)(2,1)S(1)} %get-tuple-element.66), channel_id=1, source_target_pairs={{0,8},{1,9},{2,10},{3,11},{4,12},{5,13},{6,14},{7,15},{8,0},{9,1},... | collective-permute-start | bytes 393224 | tf_op jit(solution)/shard_map/ppermute | solution.py:21
  11.7 23.3 %collective-permute-start = (bf16[512,128]{1,0:T(8,128)(2,1)S(1)}, bf16[512,128]{1,0:T(8,128)(2,1)S(1)}, u32[]{:S(2)}, u32[]{:S(2)}) collective-permute-start(bf16[512,128]{1,0:T(8,128)(2,1)S(1)} %get-tuple-element.54), channel_id=1, source_target_pairs={{0,8},{1,9},{2,10},{3,11},{4,12},{5,13},{6,14},{7,15},{8,0},{9,1},... | collective-permute-start | bytes 393224 | tf_op jit(solution)/shard_map/ppermute | solution.py:21
  22.2 4.0 %copy-start = (bf16[5,1024,1024]{2,1,0:T(8,128)(2,1)S(1)}, bf16[5,1024,1024]{2,1,0:T(8,128)(2,1)}, u32[]{:S(2)}) copy-start(bf16[5,1024,1024]{2,1,0:T(8,128)(2,1)} %transfer.39) | copy-start | bytes 31457284
  26.2 4.0 %copy-start.1 = (bf16[5,1024,1024]{2,1,0:T(8,128)(2,1)S(1)}, bf16[5,1024,1024]{2,1,0:T(8,128)(2,1)}, u32[]{:S(2)}) copy-start(bf16[5,1024,1024]{2,1,0:T(8,128)(2,1)} %transfer.39) | copy-start | bytes 31457284
  27.5 8.9 %collective-permute-start.22 = (bf16[512,128]{1,0:T(8,128)(2,1)S(1)}, bf16[512,128]{1,0:T(8,128)(2,1)S(1)}, u32[]{:S(2)}, u32[]{:S(2)}) collective-permute-start(bf16[512,128]{1,0:T(8,128)(2,1)S(1)} %get-tuple-element.92), channel_id=1, source_target_pairs={{0,4},{1,5},{2,6},{3,7},{4,0},{5,1},{6,2},{7,3},{8,12},{9,13},{10,... | collective-permute-start | bytes 393224 | tf_op jit(solution)/shard_map/ppermute | solution.py:21
  31.5 8.2 %collective-permute-start.15 = (bf16[512,128]{1,0:T(8,128)(2,1)S(1)}, bf16[512,128]{1,0:T(8,128)(2,1)S(1)}, u32[]{:S(2)}, u32[]{:S(2)}) collective-permute-start(bf16[512,128]{1,0:T(8,128)(2,1)S(1)} %get-tuple-element.80), channel_id=1, source_target_pairs={{0,4},{1,5},{2,6},{3,7},{4,0},{5,1},{6,2},{7,3},{8,12},{9,13},{10,... | collective-permute-start | bytes 393224 | tf_op jit(solution)/shard_map/ppermute | solution.py:21
  33.0 8.3 %collective-permute-start.8 = (bf16[512,128]{1,0:T(8,128)(2,1)S(1)}, bf16[512,128]{1,0:T(8,128)(2,1)S(1)}, u32[]{:S(2)}, u32[]{:S(2)}) collective-permute-start(bf16[512,128]{1,0:T(8,128)(2,1)S(1)} %get-tuple-element.68), channel_id=1, source_target_pairs={{0,4},{1,5},{2,6},{3,7},{4,0},{5,1},{6,2},{7,3},{8,12},{9,13},{10,... | collective-permute-start | bytes 393224 | tf_op jit(solution)/shard_map/ppermute | solution.py:21
  36.4 8.1 %collective-permute-start.1 = (bf16[512,128]{1,0:T(8,128)(2,1)S(1)}, bf16[512,128]{1,0:T(8,128)(2,1)S(1)}, u32[]{:S(2)}, u32[]{:S(2)}) collective-permute-start(bf16[512,128]{1,0:T(8,128)(2,1)S(1)} %get-tuple-element.56), channel_id=1, source_target_pairs={{0,4},{1,5},{2,6},{3,7},{4,0},{5,1},{6,2},{7,3},{8,12},{9,13},{10,... | collective-permute-start | bytes 393224 | tf_op jit(solution)/shard_map/ppermute | solution.py:21
  37.8 8.3 %collective-permute-start.23 = (bf16[512,128]{1,0:T(8,128)(2,1)S(1)}, bf16[512,128]{1,0:T(8,128)(2,1)S(1)}, u32[]{:S(2)}, u32[]{:S(2)}) collective-permute-start(bf16[512,128]{1,0:T(8,128)(2,1)S(1)} %get-tuple-element.94), channel_id=1, source_target_pairs={{0,2},{1,3},{2,0},{3,1},{4,6},{5,7},{6,4},{7,5},{8,10},{9,11},{10,... | collective-permute-start | bytes 393224 | tf_op jit(solution)/shard_map/ppermute | solution.py:21
  41.0 6.5 %collective-permute-start.16 = (bf16[512,128]{1,0:T(8,128)(2,1)S(1)}, bf16[512,128]{1,0:T(8,128)(2,1)S(1)}, u32[]{:S(2)}, u32[]{:S(2)}) collective-permute-start(bf16[512,128]{1,0:T(8,128)(2,1)S(1)} %get-tuple-element.82), channel_id=1, source_target_pairs={{0,2},{1,3},{2,0},{3,1},{4,6},{5,7},{6,4},{7,5},{8,10},{9,11},{10,... | collective-permute-start | bytes 393224 | tf_op jit(solution)/shard_map/ppermute | solution.py:21
  42.6 7.2 %collective-permute-start.9 = (bf16[512,128]{1,0:T(8,128)(2,1)S(1)}, bf16[512,128]{1,0:T(8,128)(2,1)S(1)}, u32[]{:S(2)}, u32[]{:S(2)}) collective-permute-start(bf16[512,128]{1,0:T(8,128)(2,1)S(1)} %get-tuple-element.70), channel_id=1, source_target_pairs={{0,2},{1,3},{2,0},{3,1},{4,6},{5,7},{6,4},{7,5},{8,10},{9,11},{10,... | collective-permute-start | bytes 393224 | tf_op jit(solution)/shard_map/ppermute | solution.py:21
  45.8 5.4 %collective-permute-start.2 = (bf16[512,128]{1,0:T(8,128)(2,1)S(1)}, bf16[512,128]{1,0:T(8,128)(2,1)S(1)}, u32[]{:S(2)}, u32[]{:S(2)}) collective-permute-start(bf16[512,128]{1,0:T(8,128)(2,1)S(1)} %get-tuple-element.58), channel_id=1, source_target_pairs={{0,2},{1,3},{2,0},{3,1},{4,6},{5,7},{6,4},{7,5},{8,10},{9,11},{10,... | collective-permute-start | bytes 393224 | tf_op jit(solution)/shard_map/ppermute | solution.py:21
  47.4 5.7 %collective-permute-start.24 = (bf16[512,128]{1,0:T(8,128)(2,1)S(1)}, bf16[512,128]{1,0:T(8,128)(2,1)S(1)}, u32[]{:S(2)}, u32[]{:S(2)}) collective-permute-start(bf16[512,128]{1,0:T(8,128)(2,1)S(1)} %get-tuple-element.96), channel_id=1, source_target_pairs={{0,1},{1,0},{2,3},{3,2},{4,5},{5,4},{6,7},{7,6},{8,9},{9,8},{10,11... | collective-permute-start | bytes 393224 | tf_op jit(solution)/shard_map/ppermute | solution.py:21
  48.9 9.0 %collective-permute-start.17 = (bf16[512,128]{1,0:T(8,128)(2,1)S(1)}, bf16[512,128]{1,0:T(8,128)(2,1)S(1)}, u32[]{:S(2)}, u32[]{:S(2)}) collective-permute-start(bf16[512,128]{1,0:T(8,128)(2,1)S(1)} %get-tuple-element.84), channel_id=1, source_target_pairs={{0,1},{1,0},{2,3},{3,2},{4,5},{5,4},{6,7},{7,6},{8,9},{9,8},{10,11... | collective-permute-start | bytes 393224 | tf_op jit(solution)/shard_map/ppermute | solution.py:21
  51.2 8.1 %collective-permute-start.10 = (bf16[512,128]{1,0:T(8,128)(2,1)S(1)}, bf16[512,128]{1,0:T(8,128)(2,1)S(1)}, u32[]{:S(2)}, u32[]{:S(2)}) collective-permute-start(bf16[512,128]{1,0:T(8,128)(2,1)S(1)} %get-tuple-element.72), channel_id=1, source_target_pairs={{0,1},{1,0},{2,3},{3,2},{4,5},{5,4},{6,7},{7,6},{8,9},{9,8},{10,11... | collective-permute-start | bytes 393224 | tf_op jit(solution)/shard_map/ppermute | solution.py:21
  52.6 11.2 %collective-permute-start.3 = (bf16[512,128]{1,0:T(8,128)(2,1)S(1)}, bf16[512,128]{1,0:T(8,128)(2,1)S(1)}, u32[]{:S(2)}, u32[]{:S(2)}) collective-permute-start(bf16[512,128]{1,0:T(8,128)(2,1)S(1)} %get-tuple-element.60), channel_id=1, source_target_pairs={{0,1},{1,0},{2,3},{3,2},{4,5},{5,4},{6,7},{7,6},{8,9},{9,8},{10,11... | collective-permute-start | bytes 393224 | tf_op jit(solution)/shard_map/ppermute | solution.py:21
  54.5 18.7 %collective-permute-start.25 = (bf16[512,128]{1,0:T(8,128)(2,1)S(1)}, bf16[512,128]{1,0:T(8,128)(2,1)S(1)}, u32[]{:S(2)}, u32[]{:S(2)}) collective-permute-start(bf16[512,128]{1,0:T(8,128)(2,1)S(1)} %get-tuple-element.98), channel_id=1, source_target_pairs={{0,8},{1,9},{2,10},{3,11},{4,12},{5,13},{6,14},{7,15},{8,0},{9,1},... | collective-permute-start | bytes 393224 | tf_op jit(solution)/shard_map/ppermute | solution.py:21
  59.2 16.8 %collective-permute-start.18 = (bf16[512,128]{1,0:T(8,128)(2,1)S(1)}, bf16[512,128]{1,0:T(8,128)(2,1)S(1)}, u32[]{:S(2)}, u32[]{:S(2)}) collective-permute-start(bf16[512,128]{1,0:T(8,128)(2,1)S(1)} %get-tuple-element.86), channel_id=1, source_target_pairs={{0,8},{1,9},{2,10},{3,11},{4,12},{5,13},{6,14},{7,15},{8,0},{9,1},... | collective-permute-start | bytes 393224 | tf_op jit(solution)/shard_map/ppermute | solution.py:21
  59.3 13.9 %copy-start.4 = (s32[16]{0:T(128)S(1)}, s32[16]{0:T(128)}, u32[]{:S(2)}) copy-start(s32[16]{0:T(128)} %owners.7) | copy-start | bytes 196
  60.8 18.0 %collective-permute-start.11 = (bf16[512,128]{1,0:T(8,128)(2,1)S(1)}, bf16[512,128]{1,0:T(8,128)(2,1)S(1)}, u32[]{:S(2)}, u32[]{:S(2)}) collective-permute-start(bf16[512,128]{1,0:T(8,128)(2,1)S(1)} %get-tuple-element.74), channel_id=1, source_target_pairs={{0,8},{1,9},{2,10},{3,11},{4,12},{5,13},{6,14},{7,15},{8,0},{9,1},... | collective-permute-start | bytes 393224 | tf_op jit(solution)/shard_map/ppermute | solution.py:21
  65.1 16.1 %collective-permute-start.4 = (bf16[512,128]{1,0:T(8,128)(2,1)S(1)}, bf16[512,128]{1,0:T(8,128)(2,1)S(1)}, u32[]{:S(2)}, u32[]{:S(2)}) collective-permute-start(bf16[512,128]{1,0:T(8,128)(2,1)S(1)} %get-tuple-element.62), channel_id=1, source_target_pairs={{0,8},{1,9},{2,10},{3,11},{4,12},{5,13},{6,14},{7,15},{8,0},{9,1},... | collective-permute-start | bytes 393224 | tf_op jit(solution)/shard_map/ppermute | solution.py:21
  74.5 8.1 %collective-permute-start.26 = (bf16[2,256,128]{2,1,0:T(8,128)(2,1)S(1)}, bf16[2,256,128]{2,1,0:T(8,128)(2,1)S(1)}, u32[]{:S(2)}, u32[]{:S(2)}) collective-permute-start(bf16[2,256,128]{2,1,0:T(8,128)(2,1)S(1)} %get-tuple-element.100), channel_id=1, source_target_pairs={{0,1},{1,0},{2,3},{3,2},{4,5},{5,4},{6,7},{7,6},{8,9},{9,8},{10,11... | collective-permute-start | bytes 393224 | tf_op jit(solution)/shard_map/ppermute | solution.py:21
  77.3 6.7 %collective-permute-start.19 = (bf16[2,256,128]{2,1,0:T(8,128)(2,1)S(1)}, bf16[2,256,128]{2,1,0:T(8,128)(2,1)S(1)}, u32[]{:S(2)}, u32[]{:S(2)}) collective-permute-start(bf16[2,256,128]{2,1,0:T(8,128)(2,1)S(1)} %get-tuple-element.88), channel_id=1, source_target_pairs={{0,1},{1,0},{2,3},{3,2},{4,5},{5,4},{6,7},{7,6},{8,9},{9,8},{10,11... | collective-permute-start | bytes 393224 | tf_op jit(solution)/shard_map/ppermute | solution.py:21
  80.1 4.8 %collective-permute-start.12 = (bf16[2,256,128]{2,1,0:T(8,128)(2,1)S(1)}, bf16[2,256,128]{2,1,0:T(8,128)(2,1)S(1)}, u32[]{:S(2)}, u32[]{:S(2)}) collective-permute-start(bf16[2,256,128]{2,1,0:T(8,128)(2,1)S(1)} %get-tuple-element.76), channel_id=1, source_target_pairs={{0,1},{1,0},{2,3},{3,2},{4,5},{5,4},{6,7},{7,6},{8,9},{9,8},{10,11... | collective-permute-start | bytes 393224 | tf_op jit(solution)/shard_map/ppermute | solution.py:21
  82.5 3.7 %collective-permute-start.5 = (bf16[2,256,128]{2,1,0:T(8,128)(2,1)S(1)}, bf16[2,256,128]{2,1,0:T(8,128)(2,1)S(1)}, u32[]{:S(2)}, u32[]{:S(2)}) collective-permute-start(bf16[2,256,128]{2,1,0:T(8,128)(2,1)S(1)} %get-tuple-element.64), channel_id=1, source_target_pairs={{0,1},{1,0},{2,3},{3,2},{4,5},{5,4},{6,7},{7,6},{8,9},{9,8},{10,11... | collective-permute-start | bytes 393224 | tf_op jit(solution)/shard_map/ppermute | solution.py:21
  82.7 4.9 %collective-permute-start.27 = (bf16[256,128]{1,0:T(8,128)(2,1)S(1)}, bf16[256,128]{1,0:T(8,128)(2,1)S(1)}, u32[]{:S(2)}, u32[]{:S(2)}) collective-permute-start(bf16[256,128]{1,0:T(8,128)(2,1)S(1)} %fusion.11), channel_id=1, source_target_pairs={{0,2},{1,3},{2,0},{3,1},{4,6},{5,7},{6,4},{7,5},{8,10},{9,11},{10,... | collective-permute-start | bytes 196616 | tf_op jit(solution)/shard_map/ppermute | solution.py:21
  84.1 5.0 %collective-permute-start.20 = (bf16[256,128]{1,0:T(8,128)(2,1)S(1)}, bf16[256,128]{1,0:T(8,128)(2,1)S(1)}, u32[]{:S(2)}, u32[]{:S(2)}) collective-permute-start(bf16[256,128]{1,0:T(8,128)(2,1)S(1)} %fusion.10), channel_id=1, source_target_pairs={{0,2},{1,3},{2,0},{3,1},{4,6},{5,7},{6,4},{7,5},{8,10},{9,11},{10,... | collective-permute-start | bytes 196616 | tf_op jit(solution)/shard_map/ppermute | solution.py:21
  84.9 5.5 %collective-permute-start.13 = (bf16[256,128]{1,0:T(8,128)(2,1)S(1)}, bf16[256,128]{1,0:T(8,128)(2,1)S(1)}, u32[]{:S(2)}, u32[]{:S(2)}) collective-permute-start(bf16[256,128]{1,0:T(8,128)(2,1)S(1)} %fusion.9), channel_id=1, source_target_pairs={{0,2},{1,3},{2,0},{3,1},{4,6},{5,7},{6,4},{7,5},{8,10},{9,11},{10,... | collective-permute-start | bytes 196616 | tf_op jit(solution)/shard_map/ppermute | solution.py:21
  86.3 5.1 %collective-permute-start.6 = (bf16[256,128]{1,0:T(8,128)(2,1)S(1)}, bf16[256,128]{1,0:T(8,128)(2,1)S(1)}, u32[]{:S(2)}, u32[]{:S(2)}) collective-permute-start(bf16[256,128]{1,0:T(8,128)(2,1)S(1)} %fusion.8), channel_id=1, source_target_pairs={{0,2},{1,3},{2,0},{3,1},{4,6},{5,7},{6,4},{7,5},{8,10},{9,11},{10,... | collective-permute-start | bytes 196616 | tf_op jit(solution)/shard_map/ppermute | solution.py:21

commit v2 on v1

v2 whole, which is shorter than its diff:
```python
import functools

import jax
import jax.numpy as jnp
from jax import lax
from jax.experimental import pallas as pl
from jax.experimental.pallas import tpu as pltpu
from jax.sharding import PartitionSpec as P

CHUNK = 128
SUB = 8
TILES = 4
AHEAD = 2
ORDER = (0, 10, 1, 30, 20, 11, 2, 21, 12, 31, 3, 22, 13, 4, 23, 32, 14, 5, 24, 33, 15, 34, 25, 35)
GROUPS = [[0, 1], [2], [3]]
PACE = (1.0, 1.4, 1.05, 0.8, 1.55)
ANY = pl.BlockSpec(memory_space=pl.ANY)
HBM = pl.BlockSpec(memory_space=pltpu.HBM)
VMEM = pl.BlockSpec(memory_space=pltpu.VMEM)
SMEM = pl.BlockSpec(memory_space=pltpu.SMEM)
COST = pl.CostEstimate(flops=1, bytes_accessed=1, transcendentals=0)
PARAMS = pltpu.CompilerParams(vmem_limit_bytes=8 * 1024 * 1024)


def from_partner(value, axis, apart):
    mask = 2**apart
    pairs = [(source, source ^ mask) for source in range(lax.axis_size(axis))]
    return lax.ppermute(value, axis, pairs)


def bit_of(apart):
    return lax.axis_index("bfly") >> apart & 1


def masked(values, first_row, rank):
    ids = lax.broadcasted_iota(jnp.int32, values.shape, 0) + first_row
    return jnp.where(ids < rank[0:1, :], values, 0.0)


def split_rows(values, y, half, own, other, base):
    rows = values.shape[0]
    y[...] = values
    out = pl.ds(base, rows // 2)
    own[out, :] = y[pl.ds(half, rows // 2, stride=2), :].astype(jnp.bfloat16)
    other[out, :] = y[pl.ds(1 - half, rows // 2, stride=2), :].astype(jnp.bfloat16)


def split_chunk(apart, rank, x, y, own, other):
    rows = x.shape[0] // TILES
    half = bit_of(apart)
    for tile in range(TILES):
        values = masked(x[pl.ds(tile * rows, rows), :].astype(jnp.float32), tile * rows, rank)
        split_rows(values, y.at[tile], half, own, other, tile * rows // 2)


def columns(ref, chunk):
    return ref.at[:, pl.ds(chunk * CHUNK, CHUNK)]


def first_kernel(apart, chunk, ranks, owners, coefficients, spread_ranks, spread_owners, own, other, rank_s, owner_s, x, y, sems):
    copies = [
        pltpu.make_async_copy(ranks, rank_s, sems.at[0]),
        pltpu.make_async_copy(owners, owner_s, sems.at[1]),
        pltpu.make_async_copy(columns(coefficients, chunk), x, sems.at[2]),
    ]
    for copy in copies:
        copy.start()
    for copy in copies:
        copy.wait()
    position = lax.axis_index("bfly")
    for level in range(spread_ranks.shape[0]):
        spread_ranks[level] = jnp.full((SUB, CHUNK), rank_s[level], jnp.int32)
    for flip in range(spread_owners.shape[0]):
        spread_owners[flip] = jnp.full((SUB, CHUNK), owner_s[position ^ flip], jnp.int32)
    split_chunk(apart, spread_ranks.at[0], x, y, own, other)


def load_kernel(coefficients, transfer, after, x, *refs):
    matrices, sems = refs[:-1], refs[-1]
    copies = [pltpu.make_async_copy(coefficients, x, sems.at[len(matrices)])]
    copies += [pltpu.make_async_copy(transfer.at[i], ref, sems.at[i]) for i, ref in enumerate(matrices)]
    for copy in copies:
        copy.start()
    for copy in copies:
        copy.wait()


def chunk_kernel(apart, chunk, spread_ranks, x, after, own, other, y):
    split_chunk(apart, spread_ranks.at[0], columns(x, chunk), y, own, other)


def product(matrix, tile, rows, apart, own, received):
    half_rows = own.shape[0]
    half = bit_of(apart)
    tile_rows = pl.ds(tile * rows, rows)
    own_cols = pl.ds(pl.multiple_of(half * half_rows, half_rows), half_rows)
    peer_cols = pl.ds(pl.multiple_of((1 - half) * half_rows, half_rows), half_rows)
    values = jnp.dot(matrix[tile_rows, own_cols], own[...], preferred_element_type=jnp.float32)
    return values + jnp.dot(matrix[tile_rows, peer_cols], received[...], preferred_element_type=jnp.float32)


def level_kernel(level, apart, next_apart, spread_ranks, matrix, own, received, after, next_own, next_other, y):
    rows = matrix.shape[0] // TILES
    half = bit_of(next_apart)
    for tile in range(TILES):
        values = product(matrix, tile, rows, apart, own, received)
        values = masked(values, tile * rows, spread_ranks.at[level + 1])
        split_rows(values, y.at[tile], half, next_own, next_other, tile * rows // 2)


def last_kernel(level, apart, place, spread_ranks, spread_owners, matrix, own, received, after, *refs):
    kept, sent = refs[-2:]
    rows = matrix.shape[0] // 4
    quarters = []
    for tile in range(4):
        values = product(matrix, tile, rows, apart, own, received)
        quarters.append(masked(values, tile * rows, spread_ranks.at[level + 1]))
    for target, slot, flip in ((sent, 0, 1), (sent, 1, 3), (kept, 0, 0), (kept, 1, 2)):
        owner = spread_owners[flip][0:1, :]
        picked = quarters[0]
        for tile in range(1, 4):
            picked = jnp.where(owner == tile, quarters[tile], picked)
        target[slot, place] = picked.astype(jnp.bfloat16)


def shape(*dims):
    return jax.ShapeDtypeStruct(dims, jnp.bfloat16)


def plan(chunks, levels):
    if ORDER and (chunks, levels) == (4, 5):
        return [(step // 10, step % 10 - 1) for step in ORDER]
    steps = [(0.1 * chunk if chunk < AHEAD else 1.01, chunk, -1) for chunk in range(chunks)]
    for chunk in range(chunks):
        at = float(chunk)
        for level in range(levels):
            at += PACE[min(level, len(PACE) - 1)]
            steps.append((at, chunk, level))
    return [step[1:] for step in sorted(steps)]


def shards(coefficients, transfer, ranks, owner_map):
    rows, width = coefficients.shape
    levels = transfer.shape[0]
    half, quarter = rows // 2, rows // 4
    count = lax.axis_size("bfly")
    log_count = count.bit_length() - 1
    bits = [(log_count - 1 - level) % log_count for level in range(levels)]
    chunks = width // CHUNK
    groups = GROUPS if chunks == 4 else [[chunk] for chunk in range(chunks)]
    group_of = {chunk: group for group in groups for chunk in group}
    strip = pltpu.VMEM((rows, CHUNK), jnp.bfloat16)
    tiles = pltpu.VMEM((TILES, rows // TILES, CHUNK), jnp.float32)
    in_hbm = functools.partial(pltpu.with_memory_space_constraint, memory_space=pltpu.HBM)
    coefficients, transfer = in_hbm(coefficients), in_hbm(transfer)

    spread_ranks, spread_owners, first_own, first_other = pl.pallas_call(
        functools.partial(first_kernel, bits[0], 0),
        out_shape=[jax.ShapeDtypeStruct((n, SUB, CHUNK), jnp.int32) for n in (levels + 1, 4)] + [shape(half, CHUNK)] * 2,
        in_specs=[HBM, HBM, HBM],
        out_specs=[VMEM] * 4,
        scratch_shapes=[
            pltpu.SMEM((levels + 1,), jnp.int32),
            pltpu.SMEM((count,), jnp.int32),
            strip,
            tiles,
            pltpu.SemaphoreType.DMA((3,)),
        ],
        cost_estimate=COST,
        compiler_params=PARAMS,
    )(in_hbm(ranks.reshape(-1)), in_hbm(owner_map), coefficients)
    x, *matrices = pl.pallas_call(
        load_kernel,
        out_shape=[shape(rows, width)] + [shape(rows, rows)] * levels,
        in_specs=[HBM, HBM, ANY],
        out_specs=[VMEM] * (levels + 1),
        scratch_shapes=[pltpu.SemaphoreType.DMA((levels + 1,))],
        cost_estimate=COST,
        compiler_params=PARAMS,
    )(coefficients, transfer, first_own)

    own, received = [None] * chunks, [None] * chunks
    ends, sums, done = {}, {}, set()
    after = x
    for chunk, level in plan(chunks, levels):
        if level + 1 < levels:
            if level < 0 and chunk == 0:
                own[chunk], other = first_own, first_other
            elif level < 0:
                own[chunk], other = pl.pallas_call(
                    functools.partial(chunk_kernel, bits[0], chunk),
                    out_shape=[shape(half, CHUNK)] * 2,
                    in_specs=[VMEM, VMEM, ANY],
                    out_specs=[VMEM, VMEM],
                    scratch_shapes=[tiles],
                    cost_estimate=COST,
                    compiler_params=PARAMS,
                )(spread_ranks, x, after)
                after = own[chunk]
            else:
                own[chunk], other = pl.pallas_call(
                    functools.partial(level_kernel, level, bits[level], bits[level + 1]),
                    out_shape=[shape(half, CHUNK)] * 2,
                    in_specs=[VMEM, VMEM, VMEM, VMEM, ANY],
                    out_specs=[VMEM, VMEM],
                    scratch_shapes=[tiles],
                    cost_estimate=COST,
                    compiler_params=PARAMS,
                )(spread_ranks, matrices[level], own[chunk], received[chunk], after)
                after = own[chunk]
            received[chunk] = from_partner(other, "bfly", bits[level + 1])
        else:
            group = group_of[chunk]
            held = ends.get(group[0], [])
            ends[group[0]] = kept, sent = pl.pallas_call(
                functools.partial(last_kernel, level, bits[level], group.index(chunk)),
                out_shape=[shape(2, len(group), quarter, CHUNK)] * 2,
                in_specs=[VMEM, VMEM, VMEM, VMEM, VMEM, ANY] + [ANY] * len(held),
                out_specs=[VMEM, VMEM],
                input_output_aliases={6 + i: i for i in range(len(held))},
                cost_estimate=COST,
                compiler_params=PARAMS,
            )(spread_ranks, spread_owners, matrices[level], own[chunk], received[chunk], after, *held)
            after = kept
            done.add(chunk)
            if done >= set(group):
                arrived = from_partner(sent, "bfly", 0)
                partial_sum = kept.astype(jnp.float32) + arrived.astype(jnp.float32)
                far_sum = from_partner(partial_sum[1].astype(jnp.bfloat16), "bfly", 1)
                total = (partial_sum[0] + far_sum.astype(jnp.float32)).astype(jnp.bfloat16)
                sums.update({member: total[i] for i, member in enumerate(group)})
    return jnp.concatenate([sums[chunk] for chunk in range(chunks)], axis=1)


def solution(mesh):
    in_specs = (P(("freq", "bfly"), None), P(None, ("freq", "bfly"), None), P(None, "bfly"), P())
    out_specs = P(("freq", "bfly"), None)
    return jax.shard_map(shards, mesh=mesh, in_specs=in_specs, out_specs=out_specs, check_vma=False)
```

time: 92.4 us -> 75.8 us (0.82)
  local copies, waits for them, and re-layouts: 8.5 us -> 0.05 us
  Pallas kernels: 29.2 us -> 20.9 us
  starting transfers between devices: 26.2 us -> 30.7 us
  waiting for transfers between devices: 27 us -> 22.9 us
    pallas_call x16, Pallas kernels: 21.4 us -> 12.1 us  [shards(): pl.pallas_call(functools.partial(level_kernel, level, bits[level], bits[l...]
    unnamed x10 -> x0, local copies, waits for them, and re-layouts: 8.46 us -> none
    ppermute x28 -> x26, starting transfers between devices: 26.2 us -> 30.7 us  [from_partner(): return lax.ppermute(value, axis, pairs)]
    ppermute x28 -> x26, waiting for transfers between devices: 27 us -> 22.9 us  [from_partner(): return lax.ppermute(value, axis, pairs)]
    pallas_call x8 -> x9, Pallas kernels: 7.79 us -> 8.77 us  [the longest x1 4.47 us: shards(): pl.pallas_call(load_kernel, out_shape=[shape(rows, width)] + [shape(rows,...]
  transfers between devices with their start and end apart: 28 -> 26, of which waited for: 10 -> 11; matrix products, arithmetic and copies ran while one was open for 0% -> 0% of each run, Pallas kernels for 31% -> 26%
where the time goes in v2:
time: 75.8 us; the launch traced here: 75.7 us
  starting transfers between devices  30.7 us (41%)
  waiting for transfers between devices  22.9 us (30%)
  Pallas kernels  20.9 us (28%)
  other arithmetic  0.91 us (1%)
    ppermute x26, starting transfers between devices, from_partner(): return lax.ppermute(value, axis, pairs)  30.7 us
    ppermute x26, waiting for transfers between devices, from_partner(): return lax.ppermute(value, axis, pairs)  22.9 us
    pallas_call x16, Pallas kernels, shards(): pl.pallas_call(functools.partial(level_kernel, level, bits[level], bits[l...  12.1 us
    pallas_call x1, Pallas kernels, shards(): pl.pallas_call(load_kernel, out_shape=[shape(rows, width)] + [shape(rows,...  4.47 us
    pallas_call x4, Pallas kernels, shards(): pl.pallas_call(functools.partial(last_kernel, level, bits[level], group.i...  2.83 us
  transfers between devices with their start and end apart: 26, of which 11 were waited for; matrix products, arithmetic and copies ran while one was open for 0% of the time, Pallas kernels for 26%

profile of v2, /device:TPU:0, one launch (start us, length us, event | category | flops | bytes accessed | tf_op | source)
XLA Modules:
  0.0 75.7 jit_solution(1373466625874862958)
XLA Ops:
  0.0 1.1 %shard_map.46 = (s32[6,8,128]{2,1,0:T(8,128)S(1)}, s32[4,8,128]{2,1,0:T(8,128)S(1)}, bf16[512,128]{1,0:T(8,128)(2,1)S(1)}, bf16[512,128]{1,0:T(8,128)(2,1)S(1)}) custom-call(s32[6]{0:T(128)} %bitcast.37, s32[16]{0:T(128)} %owners.1, bf16[1024,512]{1,0:T(8,128)(2,1)} %coefficients.3), custom_call_target="tpu_custom_call" | custom-call | flops 1 | bytes 1 | tf_op jit(solution)/shard_map/pallas_call | solution.py:157
  1.1 4.1 %collective-permute-start.1 = (bf16[512,128]{1,0:T(8,128)(2,1)S(1)}, bf16[512,128]{1,0:T(8,128)(2,1)S(1)}, u32[]{:S(2)}, u32[]{:S(2)}) collective-permute-start(bf16[512,128]{1,0:T(8,128)(2,1)S(1)} %get-tuple-element.72), channel_id=1, source_target_pairs={{0,8},{1,9},{2,10},{3,11},{4,12},{5,13},{6,14},{7,15},{8,0},{9,1},... | collective-permute-start | bytes 393224 | tf_op jit(solution)/shard_map/ppermute | solution.py:28
  5.2 4.5 %shard_map.47 = (bf16[1024,512]{1,0:T(8,128)(2,1)S(1)}, bf16[1024,1024]{1,0:T(8,128)(2,1)S(1)}, bf16[1024,1024]{1,0:T(8,128)(2,1)S(1)}, bf16[1024,1024]{1,0:T(8,...) custom-call(bf16[1024,512]{1,0:T(8,128)(2,1)} %coefficients.3, ...), custom_call_target="tpu_custom_call" | custom-call | flops 1 | bytes 1 | tf_op jit(solution)/shard_map/pallas_call | solution.py:172
  9.7 0.1 shard_map.48
  9.8 0.1 collective-permute-start
  9.9 1.6 %collective-permute-done.1.received = bf16[512,128]{1,0:T(8,128)(2,1)S(1)} collective-permute-done((bf16[512,128]{1,0:T(8,128)(2,1)S(1)}, bf16[512,128]{1,0:T(8,128)(2,1)S(1)}, u32[]{:S(2)}, u32[]{:S(2)}) %collective-permute-start.1) | collective-permute-done | bytes 131104 | tf_op jit(solution)/shard_map/ppermute | solution.py:28
  11.5 0.8 shard_map.49
  12.3 3.7 %collective-permute-start.4 = (bf16[512,128]{1,0:T(8,128)(2,1)S(1)}, bf16[512,128]{1,0:T(8,128)(2,1)S(1)}, u32[]{:S(2)}, u32[]{:S(2)}) collective-permute-start(bf16[512,128]{1,0:T(8,128)(2,1)S(1)} %get-tuple-element.79), channel_id=1, source_target_pairs={{0,4},{1,5},{2,6},{3,7},{4,0},{5,1},{6,2},{7,3},{8,12},{9,13},{10,... | collective-permute-start | bytes 393224 | tf_op jit(solution)/shard_map/ppermute | solution.py:28
  16.0 0.1 shard_map.50
  16.1 0.1 shard_map.51
  16.2 3.4 %collective-permute-start.3 = (bf16[512,128]{1,0:T(8,128)(2,1)S(1)}, bf16[512,128]{1,0:T(8,128)(2,1)S(1)}, u32[]{:S(2)}, u32[]{:S(2)}) collective-permute-start(bf16[512,128]{1,0:T(8,128)(2,1)S(1)} %get-tuple-element.78), channel_id=1, source_target_pairs={{0,8},{1,9},{2,10},{3,11},{4,12},{5,13},{6,14},{7,15},{8,0},{9,1},... | collective-permute-start | bytes 393224 | tf_op jit(solution)/shard_map/ppermute | solution.py:28
  19.7 0.7 shard_map.52
  20.4 0.1 collective-permute-start.2
  20.5 1.6 %collective-permute-start.8 = (bf16[512,128]{1,0:T(8,128)(2,1)S(1)}, bf16[512,128]{1,0:T(8,128)(2,1)S(1)}, u32[]{:S(2)}, u32[]{:S(2)}) collective-permute-start(bf16[512,128]{1,0:T(8,128)(2,1)S(1)} %get-tuple-element.86), channel_id=1, source_target_pairs={{0,8},{1,9},{2,10},{3,11},{4,12},{5,13},{6,14},{7,15},{8,0},{9,1},... | collective-permute-start | bytes 393224 | tf_op jit(solution)/shard_map/ppermute | solution.py:28
  22.1 1.6 %collective-permute-done.4.received = bf16[512,128]{1,0:T(8,128)(2,1)S(1)} collective-permute-done((bf16[512,128]{1,0:T(8,128)(2,1)S(1)}, bf16[512,128]{1,0:T(8,128)(2,1)S(1)}, u32[]{:S(2)}, u32[]{:S(2)}) %collective-permute-start.4) | collective-permute-done | bytes 131104 | tf_op jit(solution)/shard_map/ppermute | solution.py:28
  23.7 0.7 shard_map.53
  24.4 1.6 %collective-permute-start.7 = (bf16[512,128]{1,0:T(8,128)(2,1)S(1)}, bf16[512,128]{1,0:T(8,128)(2,1)S(1)}, u32[]{:S(2)}, u32[]{:S(2)}) collective-permute-start(bf16[512,128]{1,0:T(8,128)(2,1)S(1)} %get-tuple-element.85), channel_id=1, source_target_pairs={{0,2},{1,3},{2,0},{3,1},{4,6},{5,7},{6,4},{7,5},{8,10},{9,11},{10,... | collective-permute-start | bytes 393224 | tf_op jit(solution)/shard_map/ppermute | solution.py:28
  26.0 0.4 collective-permute-done.3.received
  26.4 0.7 shard_map.54
  27.1 0.7 collective-permute-start.6
  27.8 1.4 %collective-permute-done.2.received = bf16[512,128]{1,0:T(8,128)(2,1)S(1)} collective-permute-done((bf16[512,128]{1,0:T(8,128)(2,1)S(1)}, bf16[512,128]{1,0:T(8,128)(2,1)S(1)}, u32[]{:S(2)}, u32[]{:S(2)}) %collective-permute-start.2) | collective-permute-done | bytes 131104 | tf_op jit(solution)/shard_map/ppermute | solution.py:28
  29.3 0.7 shard_map.55
  30.0 2.0 %collective-permute-start.5 = (bf16[512,128]{1,0:T(8,128)(2,1)S(1)}, bf16[512,128]{1,0:T(8,128)(2,1)S(1)}, u32[]{:S(2)}, u32[]{:S(2)}) collective-permute-start(bf16[512,128]{1,0:T(8,128)(2,1)S(1)} %get-tuple-element.83), channel_id=1, source_target_pairs={{0,2},{1,3},{2,0},{3,1},{4,6},{5,7},{6,4},{7,5},{8,10},{9,11},{10,... | collective-permute-start | bytes 393224 | tf_op jit(solution)/shard_map/ppermute | solution.py:28
  32.0 0.7 shard_map.56
  32.8 0.7 shard_map.57
  33.5 0.1 collective-permute-start.12
  33.6 0.8 shard_map.58
  34.4 0.9 %collective-permute-start.11 = (bf16[512,128]{1,0:T(8,128)(2,1)S(1)}, bf16[512,128]{1,0:T(8,128)(2,1)S(1)}, u32[]{:S(2)}, u32[]{:S(2)}) collective-permute-start(bf16[512,128]{1,0:T(8,128)(2,1)S(1)} %get-tuple-element.93), channel_id=1, source_target_pairs={{0,2},{1,3},{2,0},{3,1},{4,6},{5,7},{6,4},{7,5},{8,10},{9,11},{10,... | collective-permute-start | bytes 393224 | tf_op jit(solution)/shard_map/ppermute | solution.py:28
  35.2 0.8 %collective-permute-start.10 = (bf16[512,128]{1,0:T(8,128)(2,1)S(1)}, bf16[512,128]{1,0:T(8,128)(2,1)S(1)}, u32[]{:S(2)}, u32[]{:S(2)}) collective-permute-start(bf16[512,128]{1,0:T(8,128)(2,1)S(1)} %get-tuple-element.92), channel_id=1, source_target_pairs={{0,4},{1,5},{2,6},{3,7},{4,0},{5,1},{6,2},{7,3},{8,12},{9,13},{10,... | collective-permute-start | bytes 393224 | tf_op jit(solution)/shard_map/ppermute | solution.py:28
  36.1 0.7 shard_map.59
  36.8 0.1 collective-permute-start.9
  36.9 0.7 shard_map.60
  37.6 3.0 %collective-permute-start.16 = (bf16[512,128]{1,0:T(8,128)(2,1)S(1)}, bf16[512,128]{1,0:T(8,128)(2,1)S(1)}, u32[]{:S(2)}, u32[]{:S(2)}) collective-permute-start(bf16[512,128]{1,0:T(8,128)(2,1)S(1)} %get-tuple-element.102), channel_id=1, source_target_pairs={{0,8},{1,9},{2,10},{3,11},{4,12},{5,13},{6,14},{7,15},{8,0},{9,1},... | collective-permute-start | bytes 393224 | tf_op jit(solution)/shard_map/ppermute | solution.py:28
  40.7 0.7 shard_map.61
  41.4 0.3 collective-permute-start.15
  41.7 0.7 shard_map.62
  42.4 0.6 collective-permute-start.14
  43.0 0.7 shard_map.63
  43.8 1.9 %collective-permute-start.13 = (bf16[512,128]{1,0:T(8,128)(2,1)S(1)}, bf16[512,128]{1,0:T(8,128)(2,1)S(1)}, u32[]{:S(2)}, u32[]{:S(2)}) collective-permute-start(bf16[512,128]{1,0:T(8,128)(2,1)S(1)} %get-tuple-element.99), channel_id=1, source_target_pairs={{0,8},{1,9},{2,10},{3,11},{4,12},{5,13},{6,14},{7,15},{8,0},{9,1},... | collective-permute-start | bytes 393224 | tf_op jit(solution)/shard_map/ppermute | solution.py:28
  45.7 2.1 %collective-permute-done.16.received = bf16[512,128]{1,0:T(8,128)(2,1)S(1)} collective-permute-done((bf16[512,128]{1,0:T(8,128)(2,1)S(1)}, bf16[512,128]{1,0:T(8,128)(2,1)S(1)}, u32[]{:S(2)}, u32[]{:S(2)}) %collective-permute-start.16) | collective-permute-done | bytes 131104 | tf_op jit(solution)/shard_map/ppermute | solution.py:28
  47.8 0.7 shard_map.64
  48.6 0.9 %shard_map.65 = (bf16[512,128]{1,0:T(8,128)(2,1)S(1)}, bf16[512,128]{1,0:T(8,128)(2,1)S(1)}) custom-call(s32[6,8,128]{2,1,0:T(8,128)S(1)} %get-tuple-element.61.spread_ranks, bf16[1024,1024]{1,0:T(8,128)(2,1)S(1)} %get-tuple-element.65.matrix, bf16[512,128]{1,0:T(8,128)(2,1)S(1)} %get-tuple-element.96.after.own, ...), custom_call_target="tpu_custom_call" | custom-call | flops 1 | bytes 1 | tf_op jit(solution)/shard_map/pallas_call | solution.py:201
  49.5 0.7 shard_map.66
  50.2 0.1 collective-permute-start.20
  50.3 0.5 collective-permute-start.19
  50.8 2.5 %collective-permute-done.13.received = bf16[512,128]{1,0:T(8,128)(2,1)S(1)} collective-permute-done((bf16[512,128]{1,0:T(8,128)(2,1)S(1)}, bf16[512,128]{1,0:T(8,128)(2,1)S(1)}, u32[]{:S(2)}, u32[]{:S(2)}) %collective-permute-start.13) | collective-permute-done | bytes 131104 | tf_op jit(solution)/shard_map/ppermute | solution.py:28
  53.2 0.7 shard_map.67
  54.0 0.8 shard_map.68
  54.7 0.2 collective-permute-start.23
  54.9 7.1 %collective-permute-done.19.received = bf16[512,128]{1,0:T(8,128)(2,1)S(1)} collective-permute-done((bf16[512,128]{1,0:T(8,128)(2,1)S(1)}, bf16[512,128]{1,0:T(8,128)(2,1)S(1)}, u32[]{:S(2)}, u32[]{:S(2)}) %collective-permute-start.19) | collective-permute-done | bytes 131104 | tf_op jit(solution)/shard_map/ppermute | solution.py:28
  62.0 0.7 shard_map.69
  62.7 0.1 collective-permute-start.21
  62.8 0.5 collective-permute-start.17
  63.3 1.5 %collective-permute-done.23.received = bf16[512,128]{1,0:T(8,128)(2,1)S(1)} collective-permute-done((bf16[512,128]{1,0:T(8,128)(2,1)S(1)}, bf16[512,128]{1,0:T(8,128)(2,1)S(1)}, u32[]{:S(2)}, u32[]{:S(2)}) %collective-permute-start.23) | collective-permute-done | bytes 131104 | tf_op jit(solution)/shard_map/ppermute | solution.py:28
  64.8 0.7 shard_map.70
  65.5 0.1 collective-permute-start.24
  65.7 1.9 %collective-permute-start.22 = (bf16[1,256,128]{2,1,0:T(8,128)(2,1)S(1)}, bf16[1,256,128]{2,1,0:T(8,128)(2,1)S(1)}, u32[]{:S(2)}, u32[]{:S(2)}) collective-permute-start(bf16[1,256,128]{2,1,0:T(8,128)(2,1)S(1)} %fusion.8), channel_id=1, source_target_pairs={{0,2},{1,3},{2,0},{3,1},{4,6},{5,7},{6,4},{7,5},{8,10},{9,11},{10,... | collective-permute-start | bytes 196616 | tf_op jit(solution)/shard_map/ppermute | solution.py:28
  67.6 0.1 convert_add_fusion
  67.7 0.2 collective-permute-start.18
  67.9 2.4 %collective-permute-done.22 = bf16[1,256,128]{2,1,0:T(8,128)(2,1)S(1)} collective-permute-done((bf16[1,256,128]{2,1,0:T(8,128)(2,1)S(1)}, bf16[1,256,128]{2,1,0:T(8,128)(2,1)S(1)}, u32[]{:S(2)}, u32[]{:S(2)}) %collective-permute-start.22) | collective-permute-done | bytes 65568 | tf_op jit(solution)/shard_map/ppermute | solution.py:28
  70.4 2.2 %collective-permute-start.25 = (bf16[1,256,128]{2,1,0:T(8,128)(2,1)S(1)}, bf16[1,256,128]{2,1,0:T(8,128)(2,1)S(1)}, u32[]{:S(2)}, u32[]{:S(2)}) collective-permute-start(bf16[1,256,128]{2,1,0:T(8,128)(2,1)S(1)} %fusion.10), channel_id=1, source_target_pairs={{0,2},{1,3},{2,0},{3,1},{4,6},{5,7},{6,4},{7,5},{8,10},{9,11},{10,... | collective-permute-start | bytes 196616 | tf_op jit(solution)/shard_map/ppermute | solution.py:28
  72.7 1.2 %collective-permute-done.18 = bf16[2,256,128]{2,1,0:T(8,128)(2,1)S(1)} collective-permute-done((bf16[2,256,128]{2,1,0:T(8,128)(2,1)S(1)}, bf16[2,256,128]{2,1,0:T(8,128)(2,1)S(1)}, u32[]{:S(2)}, u32[]{:S(2)}) %collective-permute-start.18) | collective-permute-done | bytes 131104 | tf_op jit(solution)/shard_map/ppermute | solution.py:28
  73.9 1.0 %collective-permute-done.25 = bf16[1,256,128]{2,1,0:T(8,128)(2,1)S(1)} collective-permute-done((bf16[1,256,128]{2,1,0:T(8,128)(2,1)S(1)}, bf16[1,256,128]{2,1,0:T(8,128)(2,1)S(1)}, u32[]{:S(2)}, u32[]{:S(2)}) %collective-permute-start.25) | collective-permute-done | bytes 65568 | tf_op jit(solution)/shard_map/ppermute | solution.py:28
  74.9 0.7 pad_maximum_fusion
  (24 shorter events, 0.2 us)
Async XLA Ops:
  1.1 10.4 %collective-permute-start.1 = (bf16[512,128]{1,0:T(8,128)(2,1)S(1)}, bf16[512,128]{1,0:T(8,128)(2,1)S(1)}, u32[]{:S(2)}, u32[]{:S(2)}) collective-permute-start(bf16[512,128]{1,0:T(8,128)(2,1)S(1)} %get-tuple-element.72), channel_id=1, source_target_pairs={{0,8},{1,9},{2,10},{3,11},{4,12},{5,13},{6,14},{7,15},{8,0},{9,1},... | collective-permute-start | bytes 393224 | tf_op jit(solution)/shard_map/ppermute | solution.py:28
  9.8 9.8 %collective-permute-start = (bf16[512,128]{1,0:T(8,128)(2,1)S(1)}, bf16[512,128]{1,0:T(8,128)(2,1)S(1)}, u32[]{:S(2)}, u32[]{:S(2)}) collective-permute-start(bf16[512,128]{1,0:T(8,128)(2,1)S(1)} %get-tuple-element.71), channel_id=1, source_target_pairs={{0,8},{1,9},{2,10},{3,11},{4,12},{5,13},{6,14},{7,15},{8,0},{9,1},... | collective-permute-start | bytes 393224 | tf_op jit(solution)/shard_map/ppermute | solution.py:28
  12.3 11.4 %collective-permute-start.4 = (bf16[512,128]{1,0:T(8,128)(2,1)S(1)}, bf16[512,128]{1,0:T(8,128)(2,1)S(1)}, u32[]{:S(2)}, u32[]{:S(2)}) collective-permute-start(bf16[512,128]{1,0:T(8,128)(2,1)S(1)} %get-tuple-element.79), channel_id=1, source_target_pairs={{0,4},{1,5},{2,6},{3,7},{4,0},{5,1},{6,2},{7,3},{8,12},{9,13},{10,... | collective-permute-start | bytes 393224 | tf_op jit(solution)/shard_map/ppermute | solution.py:28
  16.2 10.2 %collective-permute-start.3 = (bf16[512,128]{1,0:T(8,128)(2,1)S(1)}, bf16[512,128]{1,0:T(8,128)(2,1)S(1)}, u32[]{:S(2)}, u32[]{:S(2)}) collective-permute-start(bf16[512,128]{1,0:T(8,128)(2,1)S(1)} %get-tuple-element.78), channel_id=1, source_target_pairs={{0,8},{1,9},{2,10},{3,11},{4,12},{5,13},{6,14},{7,15},{8,0},{9,1},... | collective-permute-start | bytes 393224 | tf_op jit(solution)/shard_map/ppermute | solution.py:28
  20.4 8.9 %collective-permute-start.2 = (bf16[512,128]{1,0:T(8,128)(2,1)S(1)}, bf16[512,128]{1,0:T(8,128)(2,1)S(1)}, u32[]{:S(2)}, u32[]{:S(2)}) collective-permute-start(bf16[512,128]{1,0:T(8,128)(2,1)S(1)} %get-tuple-element.77), channel_id=1, source_target_pairs={{0,4},{1,5},{2,6},{3,7},{4,0},{5,1},{6,2},{7,3},{8,12},{9,13},{10,... | collective-permute-start | bytes 393224 | tf_op jit(solution)/shard_map/ppermute | solution.py:28
  20.5 11.5 %collective-permute-start.8 = (bf16[512,128]{1,0:T(8,128)(2,1)S(1)}, bf16[512,128]{1,0:T(8,128)(2,1)S(1)}, u32[]{:S(2)}, u32[]{:S(2)}) collective-permute-start(bf16[512,128]{1,0:T(8,128)(2,1)S(1)} %get-tuple-element.86), channel_id=1, source_target_pairs={{0,8},{1,9},{2,10},{3,11},{4,12},{5,13},{6,14},{7,15},{8,0},{9,1},... | collective-permute-start | bytes 393224 | tf_op jit(solution)/shard_map/ppermute | solution.py:28
  24.4 8.3 %collective-permute-start.7 = (bf16[512,128]{1,0:T(8,128)(2,1)S(1)}, bf16[512,128]{1,0:T(8,128)(2,1)S(1)}, u32[]{:S(2)}, u32[]{:S(2)}) collective-permute-start(bf16[512,128]{1,0:T(8,128)(2,1)S(1)} %get-tuple-element.85), channel_id=1, source_target_pairs={{0,2},{1,3},{2,0},{3,1},{4,6},{5,7},{6,4},{7,5},{8,10},{9,11},{10,... | collective-permute-start | bytes 393224 | tf_op jit(solution)/shard_map/ppermute | solution.py:28
  27.1 6.5 %collective-permute-start.6 = (bf16[512,128]{1,0:T(8,128)(2,1)S(1)}, bf16[512,128]{1,0:T(8,128)(2,1)S(1)}, u32[]{:S(2)}, u32[]{:S(2)}) collective-permute-start(bf16[512,128]{1,0:T(8,128)(2,1)S(1)} %get-tuple-element.84), channel_id=1, source_target_pairs={{0,4},{1,5},{2,6},{3,7},{4,0},{5,1},{6,2},{7,3},{8,12},{9,13},{10,... | collective-permute-start | bytes 393224 | tf_op jit(solution)/shard_map/ppermute | solution.py:28
  30.0 6.0 %collective-permute-start.5 = (bf16[512,128]{1,0:T(8,128)(2,1)S(1)}, bf16[512,128]{1,0:T(8,128)(2,1)S(1)}, u32[]{:S(2)}, u32[]{:S(2)}) collective-permute-start(bf16[512,128]{1,0:T(8,128)(2,1)S(1)} %get-tuple-element.83), channel_id=1, source_target_pairs={{0,2},{1,3},{2,0},{3,1},{4,6},{5,7},{6,4},{7,5},{8,10},{9,11},{10,... | collective-permute-start | bytes 393224 | tf_op jit(solution)/shard_map/ppermute | solution.py:28
  33.5 3.4 %collective-permute-start.12 = (bf16[512,128]{1,0:T(8,128)(2,1)S(1)}, bf16[512,128]{1,0:T(8,128)(2,1)S(1)}, u32[]{:S(2)}, u32[]{:S(2)}) collective-permute-start(bf16[512,128]{1,0:T(8,128)(2,1)S(1)} %get-tuple-element.94), channel_id=1, source_target_pairs={{0,1},{1,0},{2,3},{3,2},{4,5},{5,4},{6,7},{7,6},{8,9},{9,8},{10,11... | collective-permute-start | bytes 393224 | tf_op jit(solution)/shard_map/ppermute | solution.py:28
  34.4 6.3 %collective-permute-start.11 = (bf16[512,128]{1,0:T(8,128)(2,1)S(1)}, bf16[512,128]{1,0:T(8,128)(2,1)S(1)}, u32[]{:S(2)}, u32[]{:S(2)}) collective-permute-start(bf16[512,128]{1,0:T(8,128)(2,1)S(1)} %get-tuple-element.93), channel_id=1, source_target_pairs={{0,2},{1,3},{2,0},{3,1},{4,6},{5,7},{6,4},{7,5},{8,10},{9,11},{10,... | collective-permute-start | bytes 393224 | tf_op jit(solution)/shard_map/ppermute | solution.py:28
  35.2 6.4 %collective-permute-start.10 = (bf16[512,128]{1,0:T(8,128)(2,1)S(1)}, bf16[512,128]{1,0:T(8,128)(2,1)S(1)}, u32[]{:S(2)}, u32[]{:S(2)}) collective-permute-start(bf16[512,128]{1,0:T(8,128)(2,1)S(1)} %get-tuple-element.92), channel_id=1, source_target_pairs={{0,4},{1,5},{2,6},{3,7},{4,0},{5,1},{6,2},{7,3},{8,12},{9,13},{10,... | collective-permute-start | bytes 393224 | tf_op jit(solution)/shard_map/ppermute | solution.py:28
  36.8 6.2 %collective-permute-start.9 = (bf16[512,128]{1,0:T(8,128)(2,1)S(1)}, bf16[512,128]{1,0:T(8,128)(2,1)S(1)}, u32[]{:S(2)}, u32[]{:S(2)}) collective-permute-start(bf16[512,128]{1,0:T(8,128)(2,1)S(1)} %get-tuple-element.91), channel_id=1, source_target_pairs={{0,1},{1,0},{2,3},{3,2},{4,5},{5,4},{6,7},{7,6},{8,9},{9,8},{10,11... | collective-permute-start | bytes 393224 | tf_op jit(solution)/shard_map/ppermute | solution.py:28
  37.6 10.2 %collective-permute-start.16 = (bf16[512,128]{1,0:T(8,128)(2,1)S(1)}, bf16[512,128]{1,0:T(8,128)(2,1)S(1)}, u32[]{:S(2)}, u32[]{:S(2)}) collective-permute-start(bf16[512,128]{1,0:T(8,128)(2,1)S(1)} %get-tuple-element.102), channel_id=1, source_target_pairs={{0,8},{1,9},{2,10},{3,11},{4,12},{5,13},{6,14},{7,15},{8,0},{9,1},... | collective-permute-start | bytes 393224 | tf_op jit(solution)/shard_map/ppermute | solution.py:28
  41.4 7.1 %collective-permute-start.15 = (bf16[512,128]{1,0:T(8,128)(2,1)S(1)}, bf16[512,128]{1,0:T(8,128)(2,1)S(1)}, u32[]{:S(2)}, u32[]{:S(2)}) collective-permute-start(bf16[512,128]{1,0:T(8,128)(2,1)S(1)} %get-tuple-element.101), channel_id=1, source_target_pairs={{0,1},{1,0},{2,3},{3,2},{4,5},{5,4},{6,7},{7,6},{8,9},{9,8},{10,11... | collective-permute-start | bytes 393224 | tf_op jit(solution)/shard_map/ppermute | solution.py:28
  42.4 7.1 %collective-permute-start.14 = (bf16[512,128]{1,0:T(8,128)(2,1)S(1)}, bf16[512,128]{1,0:T(8,128)(2,1)S(1)}, u32[]{:S(2)}, u32[]{:S(2)}) collective-permute-start(bf16[512,128]{1,0:T(8,128)(2,1)S(1)} %get-tuple-element.100), channel_id=1, source_target_pairs={{0,2},{1,3},{2,0},{3,1},{4,6},{5,7},{6,4},{7,5},{8,10},{9,11},{10,... | collective-permute-start | bytes 393224 | tf_op jit(solution)/shard_map/ppermute | solution.py:28
  43.8 9.4 %collective-permute-start.13 = (bf16[512,128]{1,0:T(8,128)(2,1)S(1)}, bf16[512,128]{1,0:T(8,128)(2,1)S(1)}, u32[]{:S(2)}, u32[]{:S(2)}) collective-permute-start(bf16[512,128]{1,0:T(8,128)(2,1)S(1)} %get-tuple-element.99), channel_id=1, source_target_pairs={{0,8},{1,9},{2,10},{3,11},{4,12},{5,13},{6,14},{7,15},{8,0},{9,1},... | collective-permute-start | bytes 393224 | tf_op jit(solution)/shard_map/ppermute | solution.py:28
  50.2 3.7 %collective-permute-start.20 = (bf16[512,128]{1,0:T(8,128)(2,1)S(1)}, bf16[512,128]{1,0:T(8,128)(2,1)S(1)}, u32[]{:S(2)}, u32[]{:S(2)}) collective-permute-start(bf16[512,128]{1,0:T(8,128)(2,1)S(1)} %get-tuple-element.110), channel_id=1, source_target_pairs={{0,1},{1,0},{2,3},{3,2},{4,5},{5,4},{6,7},{7,6},{8,9},{9,8},{10,11... | collective-permute-start | bytes 393224 | tf_op jit(solution)/shard_map/ppermute | solution.py:28
  50.3 11.7 %collective-permute-start.19 = (bf16[512,128]{1,0:T(8,128)(2,1)S(1)}, bf16[512,128]{1,0:T(8,128)(2,1)S(1)}, u32[]{:S(2)}, u32[]{:S(2)}) collective-permute-start(bf16[512,128]{1,0:T(8,128)(2,1)S(1)} %get-tuple-element.109), channel_id=1, source_target_pairs={{0,8},{1,9},{2,10},{3,11},{4,12},{5,13},{6,14},{7,15},{8,0},{9,1},... | collective-permute-start | bytes 393224 | tf_op jit(solution)/shard_map/ppermute | solution.py:28
  54.7 10.1 %collective-permute-start.23 = (bf16[512,128]{1,0:T(8,128)(2,1)S(1)}, bf16[512,128]{1,0:T(8,128)(2,1)S(1)}, u32[]{:S(2)}, u32[]{:S(2)}) collective-permute-start(bf16[512,128]{1,0:T(8,128)(2,1)S(1)} %get-tuple-element.114), channel_id=1, source_target_pairs={{0,8},{1,9},{2,10},{3,11},{4,12},{5,13},{6,14},{7,15},{8,0},{9,1},... | collective-permute-start | bytes 393224 | tf_op jit(solution)/shard_map/ppermute | solution.py:28
  62.7 2.9 %collective-permute-start.21 = (bf16[2,1,256,128]{3,2,1,0:T(8,128)(2,1)S(1)}, bf16[2,1,256,128]{3,2,1,0:T(8,128)(2,1)S(1)}, u32[]{:S(2)}, u32[]{:S(2)}) collective-permute-start(bf16[2,1,256,128]{3,2,1,0:T(8,128)(2,1)S(1)} %get-tuple-element.113), channel_id=1, source_target_pairs={{0,1},{1,0},{2,3},{3,2},{4,5},{5,4},{6,7},{7,6},{8,9},{9,8},{10,11... | collective-permute-start | bytes 393224 | tf_op jit(solution)/shard_map/ppermute | solution.py:28
  62.8 4.8 %collective-permute-start.17 = (bf16[2,2,256,128]{3,2,1,0:T(8,128)(2,1)S(1)}, bf16[2,2,256,128]{3,2,1,0:T(8,128)(2,1)S(1)}, u32[]{:S(2)}, u32[]{:S(2)}) collective-permute-start(bf16[2,2,256,128]{3,2,1,0:T(8,128)(2,1)S(1)} %get-tuple-element.108), channel_id=1, source_target_pairs={{0,1},{1,0},{2,3},{3,2},{4,5},{5,4},{6,7},{7,6},{8,9},{9,8},{10,11... | collective-permute-start | bytes 786440 | tf_op jit(solution)/shard_map/ppermute | solution.py:28
  65.5 4.9 %collective-permute-start.24 = (bf16[2,1,256,128]{3,2,1,0:T(8,128)(2,1)S(1)}, bf16[2,1,256,128]{3,2,1,0:T(8,128)(2,1)S(1)}, u32[]{:S(2)}, u32[]{:S(2)}) collective-permute-start(bf16[2,1,256,128]{3,2,1,0:T(8,128)(2,1)S(1)} %get-tuple-element.116), channel_id=1, source_target_pairs={{0,1},{1,0},{2,3},{3,2},{4,5},{5,4},{6,7},{7,6},{8,9},{9,8},{10,11... | collective-permute-start | bytes 393224 | tf_op jit(solution)/shard_map/ppermute | solution.py:28
  65.7 4.7 %collective-permute-start.22 = (bf16[1,256,128]{2,1,0:T(8,128)(2,1)S(1)}, bf16[1,256,128]{2,1,0:T(8,128)(2,1)S(1)}, u32[]{:S(2)}, u32[]{:S(2)}) collective-permute-start(bf16[1,256,128]{2,1,0:T(8,128)(2,1)S(1)} %fusion.8), channel_id=1, source_target_pairs={{0,2},{1,3},{2,0},{3,1},{4,6},{5,7},{6,4},{7,5},{8,10},{9,11},{10,... | collective-permute-start | bytes 196616 | tf_op jit(solution)/shard_map/ppermute | solution.py:28
  67.7 6.1 %collective-permute-start.18 = (bf16[2,256,128]{2,1,0:T(8,128)(2,1)S(1)}, bf16[2,256,128]{2,1,0:T(8,128)(2,1)S(1)}, u32[]{:S(2)}, u32[]{:S(2)}) collective-permute-start(bf16[2,256,128]{2,1,0:T(8,128)(2,1)S(1)} %fusion.2), channel_id=1, source_target_pairs={{0,2},{1,3},{2,0},{3,1},{4,6},{5,7},{6,4},{7,5},{8,10},{9,11},{10,... | collective-permute-start | bytes 393224 | tf_op jit(solution)/shard_map/ppermute | solution.py:28
  70.4 4.5 %collective-permute-start.25 = (bf16[1,256,128]{2,1,0:T(8,128)(2,1)S(1)}, bf16[1,256,128]{2,1,0:T(8,128)(2,1)S(1)}, u32[]{:S(2)}, u32[]{:S(2)}) collective-permute-start(bf16[1,256,128]{2,1,0:T(8,128)(2,1)S(1)} %fusion.10), channel_id=1, source_target_pairs={{0,2},{1,3},{2,0},{3,1},{4,6},{5,7},{6,4},{7,5},{8,10},{9,11},{10,... | collective-permute-start | bytes 196616 | tf_op jit(solution)/shard_map/ppermute | solution.py:28

commit v3 on v2

--- a/solution.py
+++ b/solution.py
@@ -13,6 +13,7 @@
 AHEAD = 2
 ORDER = (0, 10, 1, 30, 20, 11, 2, 21, 12, 31, 3, 22, 13, 4, 23, 32, 14, 5, 24, 33, 15, 34, 25, 35)
 GROUPS = [[0, 1], [2], [3]]
+EARLY = (1, 2)
 PACE = (1.0, 1.4, 1.05, 0.8, 1.55)
 ANY = pl.BlockSpec(memory_space=pl.ANY)
 HBM = pl.BlockSpec(memory_space=pltpu.HBM)
@@ -89,13 +90,22 @@
     split_chunk(apart, spread_ranks.at[0], columns(x, chunk), y, own, other)
 
 
+def own_kernel(apart, matrix, own, after, total):
+    half_rows = own.shape[0]
+    own_cols = pl.ds(pl.multiple_of(bit_of(apart) * half_rows, half_rows), half_rows)
+    total[...] = jnp.dot(matrix[:, own_cols], own[...], preferred_element_type=jnp.float32)
+
+
 def product(matrix, tile, rows, apart, own, received):
-    half_rows = own.shape[0]
+    half_rows = received.shape[0]
     half = bit_of(apart)
     tile_rows = pl.ds(tile * rows, rows)
     own_cols = pl.ds(pl.multiple_of(half * half_rows, half_rows), half_rows)
     peer_cols = pl.ds(pl.multiple_of((1 - half) * half_rows, half_rows), half_rows)
-    values = jnp.dot(matrix[tile_rows, own_cols], own[...], preferred_element_type=jnp.float32)
+    if own.dtype == jnp.float32:
+        values = own[tile_rows, :]
+    else:
+        values = jnp.dot(matrix[tile_rows, own_cols], own[...], preferred_element_type=jnp.float32)
     return values + jnp.dot(matrix[tile_rows, peer_cols], received[...], preferred_element_type=jnp.float32)
 
 
@@ -183,6 +193,15 @@
     ends, sums, done = {}, {}, set()
     after = x
     for chunk, level in plan(chunks, levels):
+        if 10 * chunk + level + 1 in EARLY:
+            own[chunk] = after = pl.pallas_call(
+                functools.partial(own_kernel, bits[level]),
+                out_shape=jax.ShapeDtypeStruct((rows, CHUNK), jnp.float32),
+                in_specs=[VMEM, VMEM, ANY],
+                out_specs=VMEM,
+                cost_estimate=COST,
+                compiler_params=PARAMS,
+            )(matrices[level], own[chunk], after)
         if level + 1 < levels:
             if level < 0 and chunk == 0:
                 own[chunk], other = first_own, first_other

time: 75.8 us -> 75.5 us (level)
    pallas_call x0 -> x2, Pallas kernels: none -> 0.85 us  [shards(): pl.pallas_call(functools.partial(own_kernel, bits[level]), out_shape=jax....]
  transfers between devices with their start and end apart: 26 -> 26, of which waited for: 11 -> 11; matrix products, arithmetic and copies ran while one was open for 0% -> 0% of each run, Pallas kernels for 26% -> 27%
where the time goes in v3:
time: 75.5 us; the launch traced here: 75.4 us
  starting transfers between devices  30.5 us (40%)
  waiting for transfers between devices  22.5 us (30%)
  Pallas kernels  21.2 us (28%)
  other arithmetic  0.91 us (1%)
    ppermute x26, starting transfers between devices, from_partner(): return lax.ppermute(value, axis, pairs)  30.5 us
    ppermute x26, waiting for transfers between devices, from_partner(): return lax.ppermute(value, axis, pairs)  22.5 us
    pallas_call x16, Pallas kernels, shards(): pl.pallas_call(functools.partial(level_kernel, level, bits[level], bits[l...  11.6 us
    pallas_call x1, Pallas kernels, shards(): pl.pallas_call(load_kernel, out_shape=[shape(rows, width)] + [shape(rows,...  4.47 us
    pallas_call x4, Pallas kernels, shards(): pl.pallas_call(functools.partial(last_kernel, level, bits[level], group.i...  2.83 us
  transfers between devices with their start and end apart: 26, of which 11 were waited for; matrix products, arithmetic and copies ran while one was open for 0% of the time, Pallas kernels for 27%

profile of v3, /device:TPU:0, one launch (start us, length us, event | category | flops | bytes accessed | tf_op | source)
XLA Modules:
  0.0 75.4 jit_solution(7682095844016795714)
XLA Ops:
  0.0 1.1 %shard_map.46 = (s32[6,8,128]{2,1,0:T(8,128)S(1)}, s32[4,8,128]{2,1,0:T(8,128)S(1)}, bf16[512,128]{1,0:T(8,128)(2,1)S(1)}, bf16[512,128]{1,0:T(8,128)(2,1)S(1)}) custom-call(s32[6]{0:T(128)} %bitcast.37, s32[16]{0:T(128)} %owners.1, bf16[1024,512]{1,0:T(8,128)(2,1)} %coefficients.3), custom_call_target="tpu_custom_call" | custom-call | flops 1 | bytes 1 | tf_op jit(solution)/shard_map/pallas_call | solution.py:167
  1.1 4.1 %collective-permute-start.1 = (bf16[512,128]{1,0:T(8,128)(2,1)S(1)}, bf16[512,128]{1,0:T(8,128)(2,1)S(1)}, u32[]{:S(2)}, u32[]{:S(2)}) collective-permute-start(bf16[512,128]{1,0:T(8,128)(2,1)S(1)} %get-tuple-element.72), channel_id=1, source_target_pairs={{0,8},{1,9},{2,10},{3,11},{4,12},{5,13},{6,14},{7,15},{8,0},{9,1},... | collective-permute-start | bytes 393224 | tf_op jit(solution)/shard_map/ppermute | solution.py:29
  5.2 4.5 %shard_map.47 = (bf16[1024,512]{1,0:T(8,128)(2,1)S(1)}, bf16[1024,1024]{1,0:T(8,128)(2,1)S(1)}, bf16[1024,1024]{1,0:T(8,128)(2,1)S(1)}, bf16[1024,1024]{1,0:T(8,...) custom-call(bf16[1024,512]{1,0:T(8,128)(2,1)} %coefficients.3, ...), custom_call_target="tpu_custom_call" | custom-call | flops 1 | bytes 1 | tf_op jit(solution)/shard_map/pallas_call | solution.py:182
  9.7 0.1 shard_map.48
  9.8 0.1 collective-permute-start
  9.9 0.4 shard_map.49.own.after
  10.3 1.2 %collective-permute-done.1.received = bf16[512,128]{1,0:T(8,128)(2,1)S(1)} collective-permute-done((bf16[512,128]{1,0:T(8,128)(2,1)S(1)}, bf16[512,128]{1,0:T(8,128)(2,1)S(1)}, u32[]{:S(2)}, u32[]{:S(2)}) %collective-permute-start.1) | collective-permute-done | bytes 131104 | tf_op jit(solution)/shard_map/ppermute | solution.py:29
  11.5 0.5 shard_map.50
  12.0 3.7 %collective-permute-start.4 = (bf16[512,128]{1,0:T(8,128)(2,1)S(1)}, bf16[512,128]{1,0:T(8,128)(2,1)S(1)}, u32[]{:S(2)}, u32[]{:S(2)}) collective-permute-start(bf16[512,128]{1,0:T(8,128)(2,1)S(1)} %get-tuple-element.79), channel_id=1, source_target_pairs={{0,4},{1,5},{2,6},{3,7},{4,0},{5,1},{6,2},{7,3},{8,12},{9,13},{10,... | collective-permute-start | bytes 393224 | tf_op jit(solution)/shard_map/ppermute | solution.py:29
  15.7 0.1 shard_map.51
  15.8 0.1 shard_map.52
  15.9 3.4 %collective-permute-start.3 = (bf16[512,128]{1,0:T(8,128)(2,1)S(1)}, bf16[512,128]{1,0:T(8,128)(2,1)S(1)}, u32[]{:S(2)}, u32[]{:S(2)}) collective-permute-start(bf16[512,128]{1,0:T(8,128)(2,1)S(1)} %get-tuple-element.78), channel_id=1, source_target_pairs={{0,8},{1,9},{2,10},{3,11},{4,12},{5,13},{6,14},{7,15},{8,0},{9,1},... | collective-permute-start | bytes 393224 | tf_op jit(solution)/shard_map/ppermute | solution.py:29
  19.4 0.7 shard_map.53
  20.1 0.1 collective-permute-start.2
  20.2 1.8 %collective-permute-start.8 = (bf16[512,128]{1,0:T(8,128)(2,1)S(1)}, bf16[512,128]{1,0:T(8,128)(2,1)S(1)}, u32[]{:S(2)}, u32[]{:S(2)}) collective-permute-start(bf16[512,128]{1,0:T(8,128)(2,1)S(1)} %get-tuple-element.86), channel_id=1, source_target_pairs={{0,8},{1,9},{2,10},{3,11},{4,12},{5,13},{6,14},{7,15},{8,0},{9,1},... | collective-permute-start | bytes 393224 | tf_op jit(solution)/shard_map/ppermute | solution.py:29
  22.0 0.4 shard_map.54.own.after
  22.5 1.0 %collective-permute-done.4.received = bf16[512,128]{1,0:T(8,128)(2,1)S(1)} collective-permute-done((bf16[512,128]{1,0:T(8,128)(2,1)S(1)}, bf16[512,128]{1,0:T(8,128)(2,1)S(1)}, u32[]{:S(2)}, u32[]{:S(2)}) %collective-permute-start.4) | collective-permute-done | bytes 131104 | tf_op jit(solution)/shard_map/ppermute | solution.py:29
  23.5 0.5 shard_map.55
  24.0 1.6 %collective-permute-start.7 = (bf16[512,128]{1,0:T(8,128)(2,1)S(1)}, bf16[512,128]{1,0:T(8,128)(2,1)S(1)}, u32[]{:S(2)}, u32[]{:S(2)}) collective-permute-start(bf16[512,128]{1,0:T(8,128)(2,1)S(1)} %get-tuple-element.85), channel_id=1, source_target_pairs={{0,2},{1,3},{2,0},{3,1},{4,6},{5,7},{6,4},{7,5},{8,10},{9,11},{10,... | collective-permute-start | bytes 393224 | tf_op jit(solution)/shard_map/ppermute | solution.py:29
  25.6 0.6 collective-permute-done.3.received
  26.1 0.7 shard_map.56
  26.9 0.7 collective-permute-start.6
  27.6 1.9 %collective-permute-done.2.received = bf16[512,128]{1,0:T(8,128)(2,1)S(1)} collective-permute-done((bf16[512,128]{1,0:T(8,128)(2,1)S(1)}, bf16[512,128]{1,0:T(8,128)(2,1)S(1)}, u32[]{:S(2)}, u32[]{:S(2)}) %collective-permute-start.2) | collective-permute-done | bytes 131104 | tf_op jit(solution)/shard_map/ppermute | solution.py:29
  29.4 0.7 shard_map.57
  30.2 1.6 %collective-permute-start.5 = (bf16[512,128]{1,0:T(8,128)(2,1)S(1)}, bf16[512,128]{1,0:T(8,128)(2,1)S(1)}, u32[]{:S(2)}, u32[]{:S(2)}) collective-permute-start(bf16[512,128]{1,0:T(8,128)(2,1)S(1)} %get-tuple-element.83), channel_id=1, source_target_pairs={{0,2},{1,3},{2,0},{3,1},{4,6},{5,7},{6,4},{7,5},{8,10},{9,11},{10,... | collective-permute-start | bytes 393224 | tf_op jit(solution)/shard_map/ppermute | solution.py:29
  31.7 0.7 shard_map.58
  32.5 0.7 shard_map.59
  33.2 0.1 collective-permute-start.12
  33.3 0.7 shard_map.60
  34.1 0.9 %collective-permute-start.11 = (bf16[512,128]{1,0:T(8,128)(2,1)S(1)}, bf16[512,128]{1,0:T(8,128)(2,1)S(1)}, u32[]{:S(2)}, u32[]{:S(2)}) collective-permute-start(bf16[512,128]{1,0:T(8,128)(2,1)S(1)} %get-tuple-element.93), channel_id=1, source_target_pairs={{0,2},{1,3},{2,0},{3,1},{4,6},{5,7},{6,4},{7,5},{8,10},{9,11},{10,... | collective-permute-start | bytes 393224 | tf_op jit(solution)/shard_map/ppermute | solution.py:29
  35.0 0.8 %collective-permute-start.10 = (bf16[512,128]{1,0:T(8,128)(2,1)S(1)}, bf16[512,128]{1,0:T(8,128)(2,1)S(1)}, u32[]{:S(2)}, u32[]{:S(2)}) collective-permute-start(bf16[512,128]{1,0:T(8,128)(2,1)S(1)} %get-tuple-element.92), channel_id=1, source_target_pairs={{0,4},{1,5},{2,6},{3,7},{4,0},{5,1},{6,2},{7,3},{8,12},{9,13},{10,... | collective-permute-start | bytes 393224 | tf_op jit(solution)/shard_map/ppermute | solution.py:29
  35.8 0.7 shard_map.61
  36.5 0.1 collective-permute-start.9
  36.6 0.7 shard_map.62
  37.4 3.0 %collective-permute-start.16 = (bf16[512,128]{1,0:T(8,128)(2,1)S(1)}, bf16[512,128]{1,0:T(8,128)(2,1)S(1)}, u32[]{:S(2)}, u32[]{:S(2)}) collective-permute-start(bf16[512,128]{1,0:T(8,128)(2,1)S(1)} %get-tuple-element.102), channel_id=1, source_target_pairs={{0,8},{1,9},{2,10},{3,11},{4,12},{5,13},{6,14},{7,15},{8,0},{9,1},... | collective-permute-start | bytes 393224 | tf_op jit(solution)/shard_map/ppermute | solution.py:29
  40.4 0.7 shard_map.63
  41.1 0.3 collective-permute-start.15
  41.4 0.8 shard_map.64
  42.2 0.6 collective-permute-start.14
  42.8 0.7 shard_map.65
  43.5 1.9 %collective-permute-start.13 = (bf16[512,128]{1,0:T(8,128)(2,1)S(1)}, bf16[512,128]{1,0:T(8,128)(2,1)S(1)}, u32[]{:S(2)}, u32[]{:S(2)}) collective-permute-start(bf16[512,128]{1,0:T(8,128)(2,1)S(1)} %get-tuple-element.99), channel_id=1, source_target_pairs={{0,8},{1,9},{2,10},{3,11},{4,12},{5,13},{6,14},{7,15},{8,0},{9,1},... | collective-permute-start | bytes 393224 | tf_op jit(solution)/shard_map/ppermute | solution.py:29
  45.4 2.1 %collective-permute-done.16.received = bf16[512,128]{1,0:T(8,128)(2,1)S(1)} collective-permute-done((bf16[512,128]{1,0:T(8,128)(2,1)S(1)}, bf16[512,128]{1,0:T(8,128)(2,1)S(1)}, u32[]{:S(2)}, u32[]{:S(2)}) %collective-permute-start.16) | collective-permute-done | bytes 131104 | tf_op jit(solution)/shard_map/ppermute | solution.py:29
  47.6 0.7 shard_map.66
  48.3 0.9 %shard_map.67 = (bf16[512,128]{1,0:T(8,128)(2,1)S(1)}, bf16[512,128]{1,0:T(8,128)(2,1)S(1)}) custom-call(s32[6,8,128]{2,1,0:T(8,128)S(1)} %get-tuple-element.61.spread_ranks, bf16[1024,1024]{1,0:T(8,128)(2,1)S(1)} %get-tuple-element.65.matrix, bf16[512,128]{1,0:T(8,128)(2,1)S(1)} %get-tuple-element.96.after.own, ...), custom_call_target="tpu_custom_call" | custom-call | flops 1 | bytes 1 | tf_op jit(solution)/shard_map/pallas_call | solution.py:220
  49.2 0.7 shard_map.68
  50.1 0.4 collective-permute-start.19
  50.5 2.5 %collective-permute-done.13.received = bf16[512,128]{1,0:T(8,128)(2,1)S(1)} collective-permute-done((bf16[512,128]{1,0:T(8,128)(2,1)S(1)}, bf16[512,128]{1,0:T(8,128)(2,1)S(1)}, u32[]{:S(2)}, u32[]{:S(2)}) %collective-permute-start.13) | collective-permute-done | bytes 131104 | tf_op jit(solution)/shard_map/ppermute | solution.py:29
  53.0 0.7 shard_map.69
  53.7 0.8 %shard_map.70 = (bf16[512,128]{1,0:T(8,128)(2,1)S(1)}, bf16[512,128]{1,0:T(8,128)(2,1)S(1)}) custom-call(s32[6,8,128]{2,1,0:T(8,128)S(1)} %get-tuple-element.61.spread_ranks, bf16[1024,1024]{1,0:T(8,128)(2,1)S(1)} %get-tuple-element.65.matrix, bf16[512,128]{1,0:T(8,128)(2,1)S(1)} %get-tuple-element.105.after.own, ...), custom_call_target="tpu_custom_call" | custom-call | flops 1 | bytes 1 | tf_op jit(solution)/shard_map/pallas_call | solution.py:220
  54.5 0.1 collective-permute-start.23
  54.6 7.2 %collective-permute-done.19.received = bf16[512,128]{1,0:T(8,128)(2,1)S(1)} collective-permute-done((bf16[512,128]{1,0:T(8,128)(2,1)S(1)}, bf16[512,128]{1,0:T(8,128)(2,1)S(1)}, u32[]{:S(2)}, u32[]{:S(2)}) %collective-permute-start.19) | collective-permute-done | bytes 131104 | tf_op jit(solution)/shard_map/ppermute | solution.py:29
  61.8 0.7 shard_map.71
  62.5 0.1 collective-permute-start.21
  62.6 0.5 collective-permute-start.17
  63.0 1.5 %collective-permute-done.23.received = bf16[512,128]{1,0:T(8,128)(2,1)S(1)} collective-permute-done((bf16[512,128]{1,0:T(8,128)(2,1)S(1)}, bf16[512,128]{1,0:T(8,128)(2,1)S(1)}, u32[]{:S(2)}, u32[]{:S(2)}) %collective-permute-start.23) | collective-permute-done | bytes 131104 | tf_op jit(solution)/shard_map/ppermute | solution.py:29
  64.5 0.7 shard_map.72
  65.2 0.1 collective-permute-start.24
  65.4 1.9 %collective-permute-start.22 = (bf16[1,256,128]{2,1,0:T(8,128)(2,1)S(1)}, bf16[1,256,128]{2,1,0:T(8,128)(2,1)S(1)}, u32[]{:S(2)}, u32[]{:S(2)}) collective-permute-start(bf16[1,256,128]{2,1,0:T(8,128)(2,1)S(1)} %fusion.8), channel_id=1, source_target_pairs={{0,2},{1,3},{2,0},{3,1},{4,6},{5,7},{6,4},{7,5},{8,10},{9,11},{10,... | collective-permute-start | bytes 196616 | tf_op jit(solution)/shard_map/ppermute | solution.py:29
  67.4 0.2 collective-permute-start.18
  67.7 2.4 %collective-permute-done.22 = bf16[1,256,128]{2,1,0:T(8,128)(2,1)S(1)} collective-permute-done((bf16[1,256,128]{2,1,0:T(8,128)(2,1)S(1)}, bf16[1,256,128]{2,1,0:T(8,128)(2,1)S(1)}, u32[]{:S(2)}, u32[]{:S(2)}) %collective-permute-start.22) | collective-permute-done | bytes 65568 | tf_op jit(solution)/shard_map/ppermute | solution.py:29
  70.2 2.2 %collective-permute-start.25 = (bf16[1,256,128]{2,1,0:T(8,128)(2,1)S(1)}, bf16[1,256,128]{2,1,0:T(8,128)(2,1)S(1)}, u32[]{:S(2)}, u32[]{:S(2)}) collective-permute-start(bf16[1,256,128]{2,1,0:T(8,128)(2,1)S(1)} %fusion.10), channel_id=1, source_target_pairs={{0,2},{1,3},{2,0},{3,1},{4,6},{5,7},{6,4},{7,5},{8,10},{9,11},{10,... | collective-permute-start | bytes 196616 | tf_op jit(solution)/shard_map/ppermute | solution.py:29
  72.4 1.1 %collective-permute-done.18 = bf16[2,256,128]{2,1,0:T(8,128)(2,1)S(1)} collective-permute-done((bf16[2,256,128]{2,1,0:T(8,128)(2,1)S(1)}, bf16[2,256,128]{2,1,0:T(8,128)(2,1)S(1)}, u32[]{:S(2)}, u32[]{:S(2)}) %collective-permute-start.18) | collective-permute-done | bytes 131104 | tf_op jit(solution)/shard_map/ppermute | solution.py:29
  73.5 1.1 %collective-permute-done.25 = bf16[1,256,128]{2,1,0:T(8,128)(2,1)S(1)} collective-permute-done((bf16[1,256,128]{2,1,0:T(8,128)(2,1)S(1)}, bf16[1,256,128]{2,1,0:T(8,128)(2,1)S(1)}, u32[]{:S(2)}, u32[]{:S(2)}) %collective-permute-start.25) | collective-permute-done | bytes 65568 | tf_op jit(solution)/shard_map/ppermute | solution.py:29
  74.6 0.7 pad_maximum_fusion
  (26 shorter events, 0.3 us)
Async XLA Ops:
  1.1 10.4 %collective-permute-start.1 = (bf16[512,128]{1,0:T(8,128)(2,1)S(1)}, bf16[512,128]{1,0:T(8,128)(2,1)S(1)}, u32[]{:S(2)}, u32[]{:S(2)}) collective-permute-start(bf16[512,128]{1,0:T(8,128)(2,1)S(1)} %get-tuple-element.72), channel_id=1, source_target_pairs={{0,8},{1,9},{2,10},{3,11},{4,12},{5,13},{6,14},{7,15},{8,0},{9,1},... | collective-permute-start | bytes 393224 | tf_op jit(solution)/shard_map/ppermute | solution.py:29
  9.8 9.6 %collective-permute-start = (bf16[512,128]{1,0:T(8,128)(2,1)S(1)}, bf16[512,128]{1,0:T(8,128)(2,1)S(1)}, u32[]{:S(2)}, u32[]{:S(2)}) collective-permute-start(bf16[512,128]{1,0:T(8,128)(2,1)S(1)} %get-tuple-element.71), channel_id=1, source_target_pairs={{0,8},{1,9},{2,10},{3,11},{4,12},{5,13},{6,14},{7,15},{8,0},{9,1},... | collective-permute-start | bytes 393224 | tf_op jit(solution)/shard_map/ppermute | solution.py:29
  12.0 11.5 %collective-permute-start.4 = (bf16[512,128]{1,0:T(8,128)(2,1)S(1)}, bf16[512,128]{1,0:T(8,128)(2,1)S(1)}, u32[]{:S(2)}, u32[]{:S(2)}) collective-permute-start(bf16[512,128]{1,0:T(8,128)(2,1)S(1)} %get-tuple-element.79), channel_id=1, source_target_pairs={{0,4},{1,5},{2,6},{3,7},{4,0},{5,1},{6,2},{7,3},{8,12},{9,13},{10,... | collective-permute-start | bytes 393224 | tf_op jit(solution)/shard_map/ppermute | solution.py:29
  15.9 10.2 %collective-permute-start.3 = (bf16[512,128]{1,0:T(8,128)(2,1)S(1)}, bf16[512,128]{1,0:T(8,128)(2,1)S(1)}, u32[]{:S(2)}, u32[]{:S(2)}) collective-permute-start(bf16[512,128]{1,0:T(8,128)(2,1)S(1)} %get-tuple-element.78), channel_id=1, source_target_pairs={{0,8},{1,9},{2,10},{3,11},{4,12},{5,13},{6,14},{7,15},{8,0},{9,1},... | collective-permute-start | bytes 393224 | tf_op jit(solution)/shard_map/ppermute | solution.py:29
  20.1 9.3 %collective-permute-start.2 = (bf16[512,128]{1,0:T(8,128)(2,1)S(1)}, bf16[512,128]{1,0:T(8,128)(2,1)S(1)}, u32[]{:S(2)}, u32[]{:S(2)}) collective-permute-start(bf16[512,128]{1,0:T(8,128)(2,1)S(1)} %get-tuple-element.77), channel_id=1, source_target_pairs={{0,4},{1,5},{2,6},{3,7},{4,0},{5,1},{6,2},{7,3},{8,12},{9,13},{10,... | collective-permute-start | bytes 393224 | tf_op jit(solution)/shard_map/ppermute | solution.py:29
  20.2 11.5 %collective-permute-start.8 = (bf16[512,128]{1,0:T(8,128)(2,1)S(1)}, bf16[512,128]{1,0:T(8,128)(2,1)S(1)}, u32[]{:S(2)}, u32[]{:S(2)}) collective-permute-start(bf16[512,128]{1,0:T(8,128)(2,1)S(1)} %get-tuple-element.86), channel_id=1, source_target_pairs={{0,8},{1,9},{2,10},{3,11},{4,12},{5,13},{6,14},{7,15},{8,0},{9,1},... | collective-permute-start | bytes 393224 | tf_op jit(solution)/shard_map/ppermute | solution.py:29
  24.0 8.5 %collective-permute-start.7 = (bf16[512,128]{1,0:T(8,128)(2,1)S(1)}, bf16[512,128]{1,0:T(8,128)(2,1)S(1)}, u32[]{:S(2)}, u32[]{:S(2)}) collective-permute-start(bf16[512,128]{1,0:T(8,128)(2,1)S(1)} %get-tuple-element.85), channel_id=1, source_target_pairs={{0,2},{1,3},{2,0},{3,1},{4,6},{5,7},{6,4},{7,5},{8,10},{9,11},{10,... | collective-permute-start | bytes 393224 | tf_op jit(solution)/shard_map/ppermute | solution.py:29
  26.9 6.5 %collective-permute-start.6 = (bf16[512,128]{1,0:T(8,128)(2,1)S(1)}, bf16[512,128]{1,0:T(8,128)(2,1)S(1)}, u32[]{:S(2)}, u32[]{:S(2)}) collective-permute-start(bf16[512,128]{1,0:T(8,128)(2,1)S(1)} %get-tuple-element.84), channel_id=1, source_target_pairs={{0,4},{1,5},{2,6},{3,7},{4,0},{5,1},{6,2},{7,3},{8,12},{9,13},{10,... | collective-permute-start | bytes 393224 | tf_op jit(solution)/shard_map/ppermute | solution.py:29
  30.2 5.6 %collective-permute-start.5 = (bf16[512,128]{1,0:T(8,128)(2,1)S(1)}, bf16[512,128]{1,0:T(8,128)(2,1)S(1)}, u32[]{:S(2)}, u32[]{:S(2)}) collective-permute-start(bf16[512,128]{1,0:T(8,128)(2,1)S(1)} %get-tuple-element.83), channel_id=1, source_target_pairs={{0,2},{1,3},{2,0},{3,1},{4,6},{5,7},{6,4},{7,5},{8,10},{9,11},{10,... | collective-permute-start | bytes 393224 | tf_op jit(solution)/shard_map/ppermute | solution.py:29
  33.2 3.4 %collective-permute-start.12 = (bf16[512,128]{1,0:T(8,128)(2,1)S(1)}, bf16[512,128]{1,0:T(8,128)(2,1)S(1)}, u32[]{:S(2)}, u32[]{:S(2)}) collective-permute-start(bf16[512,128]{1,0:T(8,128)(2,1)S(1)} %get-tuple-element.94), channel_id=1, source_target_pairs={{0,1},{1,0},{2,3},{3,2},{4,5},{5,4},{6,7},{7,6},{8,9},{9,8},{10,11... | collective-permute-start | bytes 393224 | tf_op jit(solution)/shard_map/ppermute | solution.py:29
  34.1 6.3 %collective-permute-start.11 = (bf16[512,128]{1,0:T(8,128)(2,1)S(1)}, bf16[512,128]{1,0:T(8,128)(2,1)S(1)}, u32[]{:S(2)}, u32[]{:S(2)}) collective-permute-start(bf16[512,128]{1,0:T(8,128)(2,1)S(1)} %get-tuple-element.93), channel_id=1, source_target_pairs={{0,2},{1,3},{2,0},{3,1},{4,6},{5,7},{6,4},{7,5},{8,10},{9,11},{10,... | collective-permute-start | bytes 393224 | tf_op jit(solution)/shard_map/ppermute | solution.py:29
  35.0 6.4 %collective-permute-start.10 = (bf16[512,128]{1,0:T(8,128)(2,1)S(1)}, bf16[512,128]{1,0:T(8,128)(2,1)S(1)}, u32[]{:S(2)}, u32[]{:S(2)}) collective-permute-start(bf16[512,128]{1,0:T(8,128)(2,1)S(1)} %get-tuple-element.92), channel_id=1, source_target_pairs={{0,4},{1,5},{2,6},{3,7},{4,0},{5,1},{6,2},{7,3},{8,12},{9,13},{10,... | collective-permute-start | bytes 393224 | tf_op jit(solution)/shard_map/ppermute | solution.py:29
  36.5 6.3 %collective-permute-start.9 = (bf16[512,128]{1,0:T(8,128)(2,1)S(1)}, bf16[512,128]{1,0:T(8,128)(2,1)S(1)}, u32[]{:S(2)}, u32[]{:S(2)}) collective-permute-start(bf16[512,128]{1,0:T(8,128)(2,1)S(1)} %get-tuple-element.91), channel_id=1, source_target_pairs={{0,1},{1,0},{2,3},{3,2},{4,5},{5,4},{6,7},{7,6},{8,9},{9,8},{10,11... | collective-permute-start | bytes 393224 | tf_op jit(solution)/shard_map/ppermute | solution.py:29
  37.4 10.2 %collective-permute-start.16 = (bf16[512,128]{1,0:T(8,128)(2,1)S(1)}, bf16[512,128]{1,0:T(8,128)(2,1)S(1)}, u32[]{:S(2)}, u32[]{:S(2)}) collective-permute-start(bf16[512,128]{1,0:T(8,128)(2,1)S(1)} %get-tuple-element.102), channel_id=1, source_target_pairs={{0,8},{1,9},{2,10},{3,11},{4,12},{5,13},{6,14},{7,15},{8,0},{9,1},... | collective-permute-start | bytes 393224 | tf_op jit(solution)/shard_map/ppermute | solution.py:29
  41.1 7.1 %collective-permute-start.15 = (bf16[512,128]{1,0:T(8,128)(2,1)S(1)}, bf16[512,128]{1,0:T(8,128)(2,1)S(1)}, u32[]{:S(2)}, u32[]{:S(2)}) collective-permute-start(bf16[512,128]{1,0:T(8,128)(2,1)S(1)} %get-tuple-element.101), channel_id=1, source_target_pairs={{0,1},{1,0},{2,3},{3,2},{4,5},{5,4},{6,7},{7,6},{8,9},{9,8},{10,11... | collective-permute-start | bytes 393224 | tf_op jit(solution)/shard_map/ppermute | solution.py:29
  42.2 7.0 %collective-permute-start.14 = (bf16[512,128]{1,0:T(8,128)(2,1)S(1)}, bf16[512,128]{1,0:T(8,128)(2,1)S(1)}, u32[]{:S(2)}, u32[]{:S(2)}) collective-permute-start(bf16[512,128]{1,0:T(8,128)(2,1)S(1)} %get-tuple-element.100), channel_id=1, source_target_pairs={{0,2},{1,3},{2,0},{3,1},{4,6},{5,7},{6,4},{7,5},{8,10},{9,11},{10,... | collective-permute-start | bytes 393224 | tf_op jit(solution)/shard_map/ppermute | solution.py:29
  43.5 9.4 %collective-permute-start.13 = (bf16[512,128]{1,0:T(8,128)(2,1)S(1)}, bf16[512,128]{1,0:T(8,128)(2,1)S(1)}, u32[]{:S(2)}, u32[]{:S(2)}) collective-permute-start(bf16[512,128]{1,0:T(8,128)(2,1)S(1)} %get-tuple-element.99), channel_id=1, source_target_pairs={{0,8},{1,9},{2,10},{3,11},{4,12},{5,13},{6,14},{7,15},{8,0},{9,1},... | collective-permute-start | bytes 393224 | tf_op jit(solution)/shard_map/ppermute | solution.py:29
  50.0 3.7 %collective-permute-start.20 = (bf16[512,128]{1,0:T(8,128)(2,1)S(1)}, bf16[512,128]{1,0:T(8,128)(2,1)S(1)}, u32[]{:S(2)}, u32[]{:S(2)}) collective-permute-start(bf16[512,128]{1,0:T(8,128)(2,1)S(1)} %get-tuple-element.110), channel_id=1, source_target_pairs={{0,1},{1,0},{2,3},{3,2},{4,5},{5,4},{6,7},{7,6},{8,9},{9,8},{10,11... | collective-permute-start | bytes 393224 | tf_op jit(solution)/shard_map/ppermute | solution.py:29
  50.1 11.7 %collective-permute-start.19 = (bf16[512,128]{1,0:T(8,128)(2,1)S(1)}, bf16[512,128]{1,0:T(8,128)(2,1)S(1)}, u32[]{:S(2)}, u32[]{:S(2)}) collective-permute-start(bf16[512,128]{1,0:T(8,128)(2,1)S(1)} %get-tuple-element.109), channel_id=1, source_target_pairs={{0,8},{1,9},{2,10},{3,11},{4,12},{5,13},{6,14},{7,15},{8,0},{9,1},... | collective-permute-start | bytes 393224 | tf_op jit(solution)/shard_map/ppermute | solution.py:29
  54.5 10.1 %collective-permute-start.23 = (bf16[512,128]{1,0:T(8,128)(2,1)S(1)}, bf16[512,128]{1,0:T(8,128)(2,1)S(1)}, u32[]{:S(2)}, u32[]{:S(2)}) collective-permute-start(bf16[512,128]{1,0:T(8,128)(2,1)S(1)} %get-tuple-element.114), channel_id=1, source_target_pairs={{0,8},{1,9},{2,10},{3,11},{4,12},{5,13},{6,14},{7,15},{8,0},{9,1},... | collective-permute-start | bytes 393224 | tf_op jit(solution)/shard_map/ppermute | solution.py:29
  62.5 2.9 %collective-permute-start.21 = (bf16[2,1,256,128]{3,2,1,0:T(8,128)(2,1)S(1)}, bf16[2,1,256,128]{3,2,1,0:T(8,128)(2,1)S(1)}, u32[]{:S(2)}, u32[]{:S(2)}) collective-permute-start(bf16[2,1,256,128]{3,2,1,0:T(8,128)(2,1)S(1)} %get-tuple-element.113), channel_id=1, source_target_pairs={{0,1},{1,0},{2,3},{3,2},{4,5},{5,4},{6,7},{7,6},{8,9},{9,8},{10,11... | collective-permute-start | bytes 393224 | tf_op jit(solution)/shard_map/ppermute | solution.py:29
  62.6 4.8 %collective-permute-start.17 = (bf16[2,2,256,128]{3,2,1,0:T(8,128)(2,1)S(1)}, bf16[2,2,256,128]{3,2,1,0:T(8,128)(2,1)S(1)}, u32[]{:S(2)}, u32[]{:S(2)}) collective-permute-start(bf16[2,2,256,128]{3,2,1,0:T(8,128)(2,1)S(1)} %get-tuple-element.108), channel_id=1, source_target_pairs={{0,1},{1,0},{2,3},{3,2},{4,5},{5,4},{6,7},{7,6},{8,9},{9,8},{10,11... | collective-permute-start | bytes 786440 | tf_op jit(solution)/shard_map/ppermute | solution.py:29
  65.2 4.9 %collective-permute-start.24 = (bf16[2,1,256,128]{3,2,1,0:T(8,128)(2,1)S(1)}, bf16[2,1,256,128]{3,2,1,0:T(8,128)(2,1)S(1)}, u32[]{:S(2)}, u32[]{:S(2)}) collective-permute-start(bf16[2,1,256,128]{3,2,1,0:T(8,128)(2,1)S(1)} %get-tuple-element.116), channel_id=1, source_target_pairs={{0,1},{1,0},{2,3},{3,2},{4,5},{5,4},{6,7},{7,6},{8,9},{9,8},{10,11... | collective-permute-start | bytes 393224 | tf_op jit(solution)/shard_map/ppermute | solution.py:29
  65.4 4.7 %collective-permute-start.22 = (bf16[1,256,128]{2,1,0:T(8,128)(2,1)S(1)}, bf16[1,256,128]{2,1,0:T(8,128)(2,1)S(1)}, u32[]{:S(2)}, u32[]{:S(2)}) collective-permute-start(bf16[1,256,128]{2,1,0:T(8,128)(2,1)S(1)} %fusion.8), channel_id=1, source_target_pairs={{0,2},{1,3},{2,0},{3,1},{4,6},{5,7},{6,4},{7,5},{8,10},{9,11},{10,... | collective-permute-start | bytes 196616 | tf_op jit(solution)/shard_map/ppermute | solution.py:29
  67.4 6.0 %collective-permute-start.18 = (bf16[2,256,128]{2,1,0:T(8,128)(2,1)S(1)}, bf16[2,256,128]{2,1,0:T(8,128)(2,1)S(1)}, u32[]{:S(2)}, u32[]{:S(2)}) collective-permute-start(bf16[2,256,128]{2,1,0:T(8,128)(2,1)S(1)} %fusion.2), channel_id=1, source_target_pairs={{0,2},{1,3},{2,0},{3,1},{4,6},{5,7},{6,4},{7,5},{8,10},{9,11},{10,... | collective-permute-start | bytes 393224 | tf_op jit(solution)/shard_map/ppermute | solution.py:29
  70.2 4.5 %collective-permute-start.25 = (bf16[1,256,128]{2,1,0:T(8,128)(2,1)S(1)}, bf16[1,256,128]{2,1,0:T(8,128)(2,1)S(1)}, u32[]{:S(2)}, u32[]{:S(2)}) collective-permute-start(bf16[1,256,128]{2,1,0:T(8,128)(2,1)S(1)} %fusion.10), channel_id=1, source_target_pairs={{0,2},{1,3},{2,0},{3,1},{4,6},{5,7},{6,4},{7,5},{8,10},{9,11},{10,... | collective-permute-start | bytes 196616 | tf_op jit(solution)/shard_map/ppermute | solution.py:29
